TPU v7x, 32 devices: a whole 2x2x4 slice. The times are simulated.
32 devices in a mesh: expert: 8 (over y, x, core), tensor: 4 (over z).
Axes of the slice: x: 2, y: 2, z: 4, core: 2. Of those that a mesh axis runs over, the one named last changes fastest.
Arguments:
- tokens: bfloat16 [8192, 1024], P(('expert', 'tensor')), may hold values from -6 to 6
- segment_ids: int32 [8192], P('expert'), may hold values from 0 to 2, as said below
- expert_ids: int32 [8192, 8], P(('expert', 'tensor')), may hold values from 0 to 31, as said below
- slot_ids: int32 [8192, 8], P(('expert', 'tensor')), may hold values from -1 to 63, as said below
- norm1_gain: float32 [1024], replicated, may hold values from 0.5 to 1.5
- w_query: bfloat16 [1024, 1024], P(None, 'tensor'), may hold values from -2 to 2
- w_key: bfloat16 [1024, 512], P(None, 'tensor'), may hold values from -2 to 2
- w_value: bfloat16 [1024, 512], P(None, 'tensor'), may hold values from -0.1875 to 0.1875
- w_out: bfloat16 [1024, 1024], P('tensor'), may hold values from -6 to 6
- norm2_gain: float32 [1024], replicated, may hold values from 0.5 to 1.5
- w_router: bfloat16 [1024, 32], replicated, may hold values from -0.25 to 0.25
- w_gate: bfloat16 [32, 1024, 512], P('expert', None, 'tensor'), may hold values from -0.1875 to 0.1875
- w_up: bfloat16 [32, 1024, 512], P('expert', None, 'tensor'), may hold values from -0.1875 to 0.1875
- w_down: bfloat16 [32, 512, 1024], P('expert', 'tensor'), may hold values from -6 to 6
- cotangent: bfloat16 [8192, 1024], P(('expert', 'tensor')), may hold values from -6 to 6
Outputs:
- mixed: bfloat16 [8192, 1024], P(('expert', 'tensor'))
- grad_input: float32 [8192, 1024], P(('expert', 'tensor'))
- grad_norm1: float32 [1024], replicated
- grad_query: float32 [1024, 1024], P(None, 'tensor')
- grad_key: float32 [1024, 512], P(None, 'tensor')
- grad_value: float32 [1024, 512], P(None, 'tensor')
- grad_out_proj: float32 [1024, 1024], P('tensor')
- grad_norm2: float32 [1024], replicated
- grad_router: float32 [1024, 32], replicated
- grad_gate: float32 [32, 1024, 512], P('expert', None, 'tensor')
- grad_up: float32 [32, 1024, 512], P('expert', None, 'tensor')
- grad_down: float32 [32, 512, 1024], P('expert', 'tensor')
Inputs may be any that keep to these rules, and one draw needn't show every extreme that they name: `segment_ids`: each sequence of 1024 tokens holds documents 0, 1 and 2 in order; document 0 ends within the first 256 positions of its sequence and document 2 begins within the last 256. `expert_ids`: each row names 8 different experts. `slot_ids`: in each aligned block of 256 rows, a choice's slot is the number of earlier choices of the same expert in that block, counted in order of rows and then of choices, and -1 where that number is 64 or more; some expert fills all 64 slots of every block.
All inputs are finite; a program needn't handle non-finite values.
Results may differ from a plain program's by a relative error of at most 0.018.
The roundings to bfloat16 on the way count: a program that leaves them out, or rounds other values in their place, can miss the bound.
Values may be sent and summed in bfloat16 or wider, within the bound.
A program may use at most 192 MiB of HBM per device.

v0:
```python
import jax
import jax.numpy as jnp
from jax import lax
from jax.sharding import PartitionSpec as P

HDIM = 64


EPSILON = 1e-06
RESIDUAL = 0.22
MASKED = -1e30
ATTENTION_MULTIPLIER = 0.015625


def normed(rows, gain):
    return rows * lax.rsqrt(jnp.mean(rows * rows, axis=-1, keepdims=True) + EPSILON) * gain


def rope_tables(positions, width):
    half_width = width // 2
    frequency = 10000.0 ** (-(jnp.arange(half_width, dtype=jnp.float32) * 2.0) / width)
    angles = positions[:, None] * frequency[None, :]
    cos_table = jnp.concatenate([jnp.cos(angles), jnp.cos(angles)], axis=-1)
    sine_table = jnp.concatenate([jnp.sin(angles), jnp.sin(angles)], axis=-1)
    return (cos_table[:, None, :], sine_table[:, None, :])


def rotate(head_vals, cos_table, sine_table):
    half_width = head_vals.shape[-1] // 2
    turned = jnp.concatenate([-head_vals[..., half_width:], head_vals[..., :half_width]], axis=-1)
    return head_vals * cos_table + turned * sine_table


def contract_rows(left, right):
    return lax.dot_general(
        left, right, (((0,), (0,)), ((), ())), preferred_element_type=jnp.float32
    )


def contract_cols(left, right):
    return lax.dot_general(
        left, right, (((1,), (1,)), ((), ())), preferred_element_type=jnp.float32
    )


def per_device(
    tokens,
    segment_ids,
    expert_ids,
    slot_ids,
    norm1_gain,
    w_query,
    w_key,
    w_value,
    w_out,
    norm2_gain,
    w_router,
    w_gate,
    w_up,
    w_down,
    cotangent,
):
    rows_dev, model_width = tokens.shape
    top_count = expert_ids.shape[1]
    experts = w_router.shape[1]
    capacity = rows_dev * top_count // experts
    head_dim = HDIM
    key_heads = w_key.shape[1] // head_dim
    query_heads = w_query.shape[1] // head_dim
    group_size = query_heads // key_heads
    score_scale = ATTENTION_MULTIPLIER
    length = segment_ids.shape[0]
    block_rows = min(length, 512)
    blocks = length // block_rows
    inputs_f = tokens.astype(jnp.float32)
    normed_one_f, norm_one_back = jax.vjp(normed, inputs_f, norm1_gain)
    normed_one = normed_one_f.astype(jnp.bfloat16)
    whole_rows = lax.all_gather(normed_one, "tensor", axis=0, tiled=True)
    cos_table, sine_table = rope_tables(jnp.arange(length).astype(jnp.float32), head_dim)
    query_raw = jnp.dot(whole_rows, w_query, preferred_element_type=jnp.float32).reshape(
        length, query_heads, head_dim
    )
    key_raw = jnp.dot(whole_rows, w_key, preferred_element_type=jnp.float32).reshape(
        length, key_heads, head_dim
    )
    queries = (
        rotate(query_raw, cos_table, sine_table)
        .astype(jnp.bfloat16)
        .reshape(length, key_heads, group_size, head_dim)
    )
    keys_all = rotate(key_raw, cos_table, sine_table).astype(jnp.bfloat16)
    values_all = (
        jnp.dot(whole_rows, w_value, preferred_element_type=jnp.float32)
        .astype(jnp.bfloat16)
        .reshape(length, key_heads, head_dim)
    )
    key_index = jnp.arange(length)

    def scores(query_block, row_start):
        row_index = row_start + jnp.arange(block_rows)
        seg_rows = lax.dynamic_slice_in_dim(segment_ids, row_start, block_rows)
        allowed = (row_index[:, None] >= key_index[None, :]) & (
            seg_rows[:, None] == segment_ids[None, :]
        )
        raw_scores = (
            jnp.einsum("qkgd,skd->kgqs", query_block, keys_all, preferred_element_type=jnp.float32)
            * score_scale
        )
        return jnp.where(allowed[None, None], raw_scores, MASKED)

    query_blocks = queries.reshape(blocks, block_rows, key_heads, group_size, head_dim)
    row_starts = jnp.arange(blocks, dtype=jnp.int32) * block_rows

    def forward_block(block_items):
        query_block, row_start = block_items
        logits = scores(query_block, row_start)
        peak_score = jnp.max(logits, axis=-1, keepdims=True)
        weights = jnp.exp(logits - peak_score)
        row_total = jnp.sum(weights, axis=-1, keepdims=True)
        probability = (weights / row_total).astype(jnp.bfloat16)
        mixed_heads = jnp.einsum(
            "kgqs,skd->qkgd", probability, values_all, preferred_element_type=jnp.float32
        )
        return (mixed_heads.astype(jnp.bfloat16), (peak_score + jnp.log(row_total))[..., 0])

    head_out, log_totals = lax.map(forward_block, (query_blocks, row_starts))
    head_out = head_out.reshape(length, query_heads * head_dim)
    row_part = head_out
    attn = lax.psum_scatter(
        jnp.dot(row_part, w_out, preferred_element_type=jnp.float32),
        "tensor",
        scatter_dimension=0,
        tiled=True,
    )
    residual = inputs_f + RESIDUAL * attn
    normed_two_f, norm_two_back = jax.vjp(normed, residual, norm2_gain)
    normed_two = normed_two_f.astype(jnp.bfloat16)
    router_logits = jnp.dot(normed_two, w_router, preferred_element_type=jnp.float32)
    selector = (expert_ids[:, :, None] == jnp.arange(experts)[None, None, :]).astype(jnp.float32)

    def gating(logit_rows):
        return jax.nn.softmax(jnp.sum(selector * logit_rows[:, None, :], axis=-1), axis=-1)

    gate_weights, gating_back = jax.vjp(gating, router_logits)
    target = jnp.where(slot_ids >= 0, expert_ids * capacity + slot_ids, -1).reshape(
        rows_dev * top_count
    )
    onehot = (target[:, None] == jnp.arange(experts * capacity)[None, :]).astype(jnp.bfloat16)
    row_hot = jnp.sum(onehot.reshape(rows_dev, top_count, experts * capacity), axis=1)
    outgoing = (
        contract_rows(row_hot, normed_two)
        .astype(jnp.bfloat16)
        .reshape(experts, capacity, model_width)
    )
    arrived = lax.all_to_all(outgoing, "expert", split_axis=0, concat_axis=1, tiled=True)
    gate_w, up_w, down_w = (
        lax.all_gather(w_gate, "tensor", axis=2, tiled=True),
        lax.all_gather(w_up, "tensor", axis=2, tiled=True),
        lax.all_gather(w_down, "tensor", axis=1, tiled=True),
    )
    gate_act = jnp.einsum("erd,edf->erf", arrived, gate_w, preferred_element_type=jnp.float32)
    up_act = jnp.einsum("erd,edf->erf", arrived, up_w, preferred_element_type=jnp.float32)
    sigmoid_gate = jax.nn.sigmoid(gate_act)
    swish_act = gate_act * sigmoid_gate
    hidden = (swish_act * up_act).astype(jnp.bfloat16)
    expert_terms = jnp.einsum("erf,efd->erd", hidden, down_w, preferred_element_type=jnp.float32)
    returned = lax.all_to_all(
        expert_terms.astype(jnp.bfloat16), "expert", split_axis=1, concat_axis=0, tiled=True
    )
    picked = jnp.dot(
        onehot,
        returned.reshape(experts * capacity, model_width),
        preferred_element_type=jnp.float32,
    )
    picked = picked.reshape(rows_dev, top_count, model_width)
    expert_mix = jnp.sum(gate_weights[:, :, None] * picked, axis=1)
    mixed_out = (residual + RESIDUAL * expert_mix).astype(jnp.bfloat16)
    upstream = cotangent.astype(jnp.float32)
    grad_mix = RESIDUAL * upstream
    grad_gates = jnp.sum(picked * grad_mix[:, None, :], axis=-1)
    grad_picked = (
        (gate_weights[:, :, None] * grad_mix[:, None, :])
        .astype(jnp.bfloat16)
        .reshape(rows_dev * top_count, model_width)
    )
    grad_slots = (
        contract_rows(onehot, grad_picked)
        .astype(jnp.bfloat16)
        .reshape(experts, capacity, model_width)
    )
    grad_arrived = lax.all_to_all(grad_slots, "expert", split_axis=0, concat_axis=1, tiled=True)
    grad_down_w = jnp.einsum(
        "erf,erd->efd", hidden, grad_arrived, preferred_element_type=jnp.float32
    )
    grad_hidden = jnp.einsum(
        "erd,efd->erf", grad_arrived, down_w, preferred_element_type=jnp.float32
    )
    grad_gate_act = (
        grad_hidden * up_act * (sigmoid_gate * (1.0 + gate_act * (1.0 - sigmoid_gate)))
    ).astype(jnp.bfloat16)
    grad_up_act = (grad_hidden * swish_act).astype(jnp.bfloat16)
    grad_gate_w = jnp.einsum(
        "erd,erf->edf", arrived, grad_gate_act, preferred_element_type=jnp.float32
    )
    grad_up_w = jnp.einsum("erd,erf->edf", arrived, grad_up_act, preferred_element_type=jnp.float32)
    grad_rows_in = jnp.einsum(
        "erf,edf->erd", grad_gate_act, gate_w, preferred_element_type=jnp.float32
    )
    grad_rows_in = grad_rows_in + jnp.einsum(
        "erf,edf->erd", grad_up_act, up_w, preferred_element_type=jnp.float32
    )
    grad_gate_w, grad_up_w, grad_down_w = (
        lax.psum_scatter(
            grad_gate_w.astype(jnp.bfloat16), "tensor", scatter_dimension=2, tiled=True
        ).astype(jnp.float32),
        lax.psum_scatter(
            grad_up_w.astype(jnp.bfloat16), "tensor", scatter_dimension=2, tiled=True
        ).astype(jnp.float32),
        lax.psum_scatter(
            grad_down_w.astype(jnp.bfloat16), "tensor", scatter_dimension=1, tiled=True
        ).astype(jnp.float32),
    )
    grad_returned = lax.all_to_all(
        grad_rows_in.astype(jnp.bfloat16), "expert", split_axis=1, concat_axis=0, tiled=True
    )
    grad_normed_two = jnp.dot(
        onehot,
        grad_returned.reshape(experts * capacity, model_width),
        preferred_element_type=jnp.float32,
    )
    grad_normed_two = jnp.sum(grad_normed_two.reshape(rows_dev, top_count, model_width), axis=1)
    grad_logits = gating_back(grad_gates)[0].astype(jnp.bfloat16)
    grad_router = contract_rows(normed_two, grad_logits)
    grad_normed_two = grad_normed_two + contract_cols(grad_logits, w_router)
    grad_residual, grad_norm2 = norm_two_back(grad_normed_two)
    grad_residual = grad_residual + upstream
    grad_attn = (RESIDUAL * grad_residual).astype(jnp.bfloat16)
    grad_attn_all = lax.all_gather(grad_attn, "tensor", axis=0, tiled=True)
    grad_out_w = contract_rows(head_out, grad_attn_all)
    grad_heads = contract_cols(grad_attn_all, w_out).astype(jnp.bfloat16)
    grad_heads = grad_heads.reshape(blocks, block_rows, key_heads, group_size, head_dim)

    def backward_block(carried, block_items):
        grad_keys, grad_values = carried
        query_block, row_start, log_total, grad_block = block_items
        logits = scores(query_block, row_start)
        probability = jnp.exp(logits - log_total[..., None])
        grad_values = grad_values + jnp.einsum(
            "kgqs,qkgd->skd",
            probability.astype(jnp.bfloat16),
            grad_block,
            preferred_element_type=jnp.float32,
        )
        grad_probs = jnp.einsum(
            "qkgd,skd->kgqs", grad_block, values_all, preferred_element_type=jnp.float32
        )
        centre = jnp.sum(probability * grad_probs, axis=-1, keepdims=True)
        grad_scores = (probability * (grad_probs - centre)).astype(jnp.bfloat16)
        grad_query_block = (
            jnp.einsum("kgqs,skd->qkgd", grad_scores, keys_all, preferred_element_type=jnp.float32)
            * score_scale
        )
        grad_keys = (
            grad_keys
            + jnp.einsum(
                "kgqs,qkgd->skd", grad_scores, query_block, preferred_element_type=jnp.float32
            )
            * score_scale
        )
        return ((grad_keys, grad_values), grad_query_block)

    zero_keys = jnp.zeros((length, key_heads, head_dim), jnp.float32)
    (grad_keys, grad_values), grad_queries = lax.scan(
        backward_block, (zero_keys, zero_keys), (query_blocks, row_starts, log_totals, grad_heads)
    )
    grad_queries = grad_queries.reshape(length, query_heads, head_dim)
    _, rope_query_back = jax.vjp(
        lambda head_vals: rotate(head_vals, cos_table, sine_table), query_raw
    )
    _, rope_key_back = jax.vjp(lambda head_vals: rotate(head_vals, cos_table, sine_table), key_raw)
    grad_query_raw = (
        rope_query_back(grad_queries)[0]
        .astype(jnp.bfloat16)
        .reshape(length, query_heads * head_dim)
    )
    grad_key_raw = (
        rope_key_back(grad_keys)[0].astype(jnp.bfloat16).reshape(length, key_heads * head_dim)
    )
    grad_value_raw = grad_values.astype(jnp.bfloat16).reshape(length, key_heads * head_dim)
    grad_query_w = contract_rows(whole_rows, grad_query_raw)
    grad_key_w = contract_rows(whole_rows, grad_key_raw)
    grad_value_w = contract_rows(whole_rows, grad_value_raw)

    def row_part(values_in):
        return values_in

    summed = contract_cols(row_part(grad_query_raw), w_query)
    summed = summed + contract_cols(row_part(grad_key_raw), w_key)
    grad_normed_one = lax.psum_scatter(
        (summed + contract_cols(row_part(grad_value_raw), w_value)).astype(jnp.bfloat16),
        "tensor",
        scatter_dimension=0,
        tiled=True,
    ).astype(jnp.float32)
    grad_inputs, grad_norm1 = norm_one_back(grad_normed_one)
    grad_inputs = grad_inputs + grad_residual
    grad_query_w, grad_key_w, grad_value_w, grad_out_w = (
        lax.psum(grad_query_w.astype(jnp.bfloat16), "expert").astype(jnp.float32),
        lax.psum(grad_key_w.astype(jnp.bfloat16), "expert").astype(jnp.float32),
        lax.psum(grad_value_w.astype(jnp.bfloat16), "expert").astype(jnp.float32),
        lax.psum(grad_out_w.astype(jnp.bfloat16), "expert").astype(jnp.float32),
    )
    grad_norm1, grad_norm2, grad_router = lax.psum(
        (grad_norm1, grad_norm2, grad_router), ("expert", "tensor")
    )
    return (
        mixed_out,
        grad_inputs,
        grad_norm1,
        grad_query_w,
        grad_key_w,
        grad_value_w,
        grad_out_w,
        grad_norm2,
        grad_router,
        grad_gate_w,
        grad_up_w,
        grad_down_w,
    )


def solution(mesh):
    return jax.shard_map(
        per_device,
        mesh=mesh,
        in_specs=(
            P(("expert", "tensor"), None),
            P("expert"),
            P(("expert", "tensor"), None),
            P(("expert", "tensor"), None),
            P(),
            P(None, "tensor"),
            P(None, "tensor"),
            P(None, "tensor"),
            P("tensor", None),
            P(),
            P(),
            P("expert", None, "tensor"),
            P("expert", None, "tensor"),
            P("expert", "tensor", None),
            P(("expert", "tensor"), None),
        ),
        out_specs=(
            P(("expert", "tensor"), None),
            P(("expert", "tensor"), None),
            P(),
            P(None, "tensor"),
            P(None, "tensor"),
            P(None, "tensor"),
            P("tensor", None),
            P(),
            P(),
            P("expert", None, "tensor"),
            P("expert", None, "tensor"),
            P("expert", "tensor", None),
        ),
        check_vma=False,
    )
```

profile of v0, /device:TPU:0, one launch (start us, length us, event | category | flops | bytes accessed | tf_op | source)
XLA Modules:
  0.0 1164.6 jit_solution(12330489112933008041)
XLA Ops:
  15.3 44.2 %all-gather.6.cloned.1.call-done = bf16[1024,1024]{1,0:T(8,128)(2,1)} async-done(((bf16[256,1024]{1,0:T(8,128)(2,1)}), bf16[1024,1024]{1,0:T(8,128)(2,1)}) %all-gather.6.cloned.1.call-update) | async-done | bytes 2097168 | tf_op jit(solution)/shard_map/all_gather | solution.py:78
  78.1 23.3 %while.28 = (s32[]{:T(128)}, bf16[2,512,2,2,64]{1,4,3,2,0:T(8,128)(2,1)}, f32[2,2,2,512]{3,2,1,0:T(2,128)S(1)}, s32[2]{0:T(128)S(1)}, s32[1024]{0:T(1024)S(1)}, ...) while((s32[]{:T(128)}, ...), condition=%wide.region_4.5_spmd.clone, body=%wide.region_1.4_spmd.clone.sunk | while | flops 563739136 | bytes 33634572 | solution.py:126
  108.0 10.7 fusion.64
  118.7 63.5 %reduce-scatter.10.cloned.1.call-done = f32[256,1024]{1,0:T(8,128)} async-done(((f32[1024,1024]{1,0:T(8,128)}), f32[256,1024]{1,0:T(8,128)}) %reduce-scatter.10.cloned.1.call-update) | async-done | bytes 1048592 | tf_op jit(solution)/shard_map/reduce_scatter | solution.py:129
  195.9 12.7 %fusion.73 = bf16[2048,1024]{1,0:T(8,128)(2,1)} fusion(f32[256,1024]{1,0:T(8,128)} %convert_multiply_fusion.6, f32[2048]{0:T(1024)S(1)} %div.92, s32[2048]{0:T(1024)} %eq.106), kind=kOutput, calls=%fused_computation.90 | convolution fusion | flops 8600420352 | bytes 5259264 | tf_op jit(solution)/shard_map/dot_general | solution.py:35
  208.5 32.6 %all-to-all-done = bf16[32,64,1024]{2,1,0:T(8,128)(2,1)} async-done(((bf16[32,64,1024]{2,1,0:T(8,128)(2,1)}), bf16[32,64,1024]{2,1,0:T(8,128)(2,1)}, u32[]{:S(2)}, u32[]{:S(2)}) %all-to-all-start) | async-done | bytes 4194336 | tf_op jit(solution)/shard_map/all_to_all | solution.py:155
  250.8 44.0 %all-to-all-done.2 = bf16[32,64,1024]{2,1,0:T(8,128)(2,1)} async-done(((bf16[32,64,1024]{2,1,0:T(8,128)(2,1)}), bf16[32,64,1024]{2,1,0:T(8,128)(2,1)}, u32[]{:S(2)}, u32[]{:S(2)}) %all-to-all-start.2) | async-done | bytes 4194336 | tf_op jit(solution)/shard_map/all_to_all | solution.py:191
  299.7 7.9 fusion.104
  307.7 37.6 %all-gather.8.cloned.1.call-done = bf16[4,1024,512]{2,1,0:T(8,128)(2,1)} async-done(((bf16[4,1024,128]{2,1,0:T(8,128)(2,1)}), bf16[4,1024,512]{2,1,0:T(8,128)(2,1)}) %all-gather.8.cloned.1.call-update) | async-done | bytes 4194320 | tf_op jit(solution)/shard_map/all_gather | solution.py:157
  345.2 7.8 fusion.103
  353.0 72.7 %all-gather.12.cloned.1.call-done = bf16[4,512,1024]{2,1,0:T(8,128)(2,1)} async-done(((bf16[4,128,1024]{2,1,0:T(8,128)(2,1)}), bf16[4,512,1024]{2,1,0:T(8,128)(2,1)}) %all-gather.12.cloned.1.call-update) | async-done | bytes 4194320 | tf_op jit(solution)/shard_map/all_gather | solution.py:159
  425.7 12.0 %multiply_convert_fusion = (bf16[4,512,512]{2,1,0:T(8,128)(2,1)}, bf16[4,512,512]{2,1,0:T(8,128)(2,1)}, bf16[4,512,512]{2,1,0:T(8,128)(2,1)S(1)}) fusion(f32[4,512,512]{2,1,0:T(8,128)} %fusion.103, f32[4,512,512]{2,1,0:T(8,128)} %fusion.104, bf16[4,512,1024]{2,1,0:T(8,128)(2,1)} %bitcast.304, bf16[4,512,1024]{2,1,0:T(8,128)(2,1)} %all-gather.12.cloned.1.call-done), kind=kOutput, calls=%fused_computation.84 | convolution fusion | flops 2163212288 | bytes 23068672 | tf_op jit(solution)/shard_map/erd,efd->erf/dot_general | solution.py:195
  465.9 33.3 %all-to-all-done.1 = bf16[4,512,1024]{2,0,1:T(4,128)(2,1)} async-done(((bf16[4,512,1024]{2,0,1:T(4,128)(2,1)}), bf16[4,512,1024]{2,0,1:T(4,128)(2,1)}, u32[]{:S(2)}, u32[]{:S(2)}) %all-to-all-start.1) | async-done | bytes 4194336 | tf_op jit(solution)/shard_map/all_to_all | solution.py:167
  507.6 11.1 multiply_reduce_fusion
  518.9 34.0 %all-to-all-done.3 = bf16[4,512,1024]{2,0,1:T(4,128)(2,1)} async-done(((bf16[4,512,1024]{2,0,1:T(4,128)(2,1)}), bf16[4,512,1024]{2,0,1:T(4,128)(2,1)}, u32[]{:S(2)}, u32[]{:S(2)}) %all-to-all-start.3) | async-done | bytes 4194336 | tf_op jit(solution)/shard_map/all_to_all | solution.py:223
  556.6 9.2 fusion.76
  569.3 42.7 %all-gather.14.cloned.1.call-done = bf16[1024,1024]{1,0:T(8,128)(2,1)} async-done(((bf16[256,1024]{1,0:T(8,128)(2,1)}), bf16[1024,1024]{1,0:T(8,128)(2,1)}) %all-gather.14.cloned.1.call-update) | async-done | bytes 2097168 | tf_op jit(solution)/shard_map/all_gather | solution.py:238
  618.3 55.7 %while.29 = (s32[]{:T(128)}, f32[1024,2,64]{0,2,1:T(8,128)S(1)}, f32[1024,2,64]{0,2,1:T(8,128)}, f32[2,512,2,2,64]{1,0,4,3,2:T(2,128)}, bf16[2,512,2,2,64]{1,4,3...) while((s32[]{:T(128)}, f32[1024,2,64]{0,2,1:T(8,128)S(1)}, ...), condition=%wide.region_19.20_spmd.clone, body=%wide.region_17.19_spmd.clone.sunk | while | flops 1375992320 | bytes 71637224 | solution.py:273
  635.2 10.4 dynamic_update_slice.22
  663.4 10.4 dynamic_update_slice.22
  685.4 6.6 convolution_convert_fusion.2
  692.0 8.0 copy.115
  700.1 6.6 copy.139
  708.3 6.5 convolution_convert_fusion.3
  714.8 8.3 copy.113
  731.2 6.7 convolution_convert_fusion.1
  751.3 70.7 %reduce-scatter.18.cloned.1.call-done = bf16[128,4096]{1,0:T(8,128)(2,1)} async-done(((bf16[512,4096]{1,0:T(8,128)(2,1)}), bf16[128,4096]{1,0:T(8,128)(2,1)}) %reduce-scatter.18.cloned.1.call-update) | async-done | bytes 1048592
  825.6 76.2 %reduce-scatter.16.cloned.1.call-done = bf16[128,4096]{1,0:T(8,128)(2,1)} async-done(((bf16[512,4096]{1,0:T(8,128)(2,1)}), bf16[128,4096]{1,0:T(8,128)(2,1)}) %reduce-scatter.16.cloned.1.call-update) | async-done | bytes 1048592
  908.9 72.2 %reduce-scatter.14.cloned.1.call-done = bf16[4,128,1024]{2,1,0:T(8,128)(2,1)} async-done(((bf16[4,512,1024]{2,1,0:T(8,128)(2,1)}), bf16[4,128,1024]{2,1,0:T(8,128)(2,1)}) %reduce-scatter.14.cloned.1.call-update) | async-done | bytes 1048592 | tf_op jit(solution)/shard_map/reduce_scatter | solution.py:219
  984.0 43.9 %reduce-scatter.12.cloned.1.call-done = bf16[256,1024]{1,0:T(8,128)(2,1)} async-done(((bf16[1024,1024]{1,0:T(8,128)(2,1)}), bf16[256,1024]{1,0:T(8,128)(2,1)}) %reduce-scatter.12.cloned.1.call-update) | async-done | bytes 524304 | tf_op jit(solution)/shard_map/reduce_scatter | solution.py:299
  1032.8 39.6 %all-reduce.4 = (f32[1024]{0:T(1024)}, f32[1024]{0:T(1024)}) all-reduce(f32[1024]{0:T(1024)S(1)} %get-tuple-element.257, f32[1024]{0:T(1024)S(1)} %copy-done.55), channel_id=1, replica_groups=mesh['expert'=8,'tensor'=4] {'expert','tensor'}, use_global_device_ids=true, to_apply=%region_23.24 | all-reduce | flops 2048 | bytes 16384 | tf_op jit(solution)/shard_map/psum | solution.py:313
  1072.4 83.3 %all-reduce.9.cloned.1.call-done = f32[1024,32]{0,1:T(8,128)} async-done(((f32[1024,32]{0,1:T(8,128)}), f32[1024,32]{0,1:T(8,128)}) %all-reduce.9.cloned.1.call-update) | async-done | bytes 131088 | tf_op jit(solution)/shard_map/psum | solution.py:313
  (315 shorter events, 215.3 us)
Async XLA Ops:
  7.2 96.6 %copy-start = (bf16[256,1024]{1,0:T(8,128)(2,1)S(1)}, bf16[256,1024]{1,0:T(8,128)(2,1)}, u32[]{:S(2)}) copy-start(bf16[256,1024]{1,0:T(8,128)(2,1)} %param.27) | copy-start | bytes 1572868
  7.2 52.2 %all-gather.6.cloned.1.call-start = ((), (), s32[]{:S(2)}) async-start(), calls=%async_computation.9 | async-start | bytes 2621440 | tf_op jit(solution)/shard_map/all_gather | solution.py:78
  10.7 171.5 %reduce-scatter.10.cloned.1.call-start = ((), (), s32[]{:S(2)}) async-start(), calls=%async_computation.10 | async-start | bytes 5242880 | tf_op jit(solution)/shard_map/reduce_scatter | solution.py:129
  106.5 75.7 %copy-start.6 = (bf16[256,1024]{1,0:T(8,128)(2,1)S(1)}, bf16[256,1024]{1,0:T(8,128)(2,1)}, u32[]{:S(2)}) copy-start(bf16[256,1024]{1,0:T(8,128)(2,1)} %param.19) | copy-start | bytes 1572868
  106.5 77.3 %copy-start.47 = (f32[1024]{0:T(1024)S(1)}, f32[1024]{0:T(1024)}, u32[]{:S(2)}) copy-start(f32[1024]{0:T(1024)} %param.28) | copy-start | bytes 12292
  106.6 193.2 %all-gather.10.cloned.1.call-start = ((), (), s32[]{:S(2)}) async-start(), calls=%async_computation.12 | async-start | bytes 5242880 | tf_op jit(solution)/shard_map/all_gather | solution.py:158
  107.3 237.9 %all-gather.8.cloned.1.call-start = ((), (), s32[]{:S(2)}) async-start(), calls=%async_computation.11 | async-start | bytes 5242880 | tf_op jit(solution)/shard_map/all_gather | solution.py:157
  107.9 79.4 %copy-start.50 = (s32[256,8]{0,1:T(8,128)}, s32[256,8]{0,1:T(8,128)S(1)}, u32[]{:S(2)}) copy-start(s32[256,8]{0,1:T(8,128)S(1)} %add_select_fusion) | copy-start | bytes 24580
  183.8 383.3 %copy-start.4 = (f32[256,1024]{1,0:T(8,128)}, f32[256,1024]{1,0:T(8,128)S(1)}, u32[]{:S(2)}) copy-start(f32[256,1024]{1,0:T(8,128)S(1)} %get-tuple-element.304) | copy-start | bytes 3145732
  187.3 53.8 %all-to-all-start = ((bf16[32,64,1024]{2,1,0:T(8,128)(2,1)}), bf16[32,64,1024]{2,1,0:T(8,128)(2,1)}, u32[]{:S(2)}, u32[]{:S(2)}) async-start(bf16[32,64,1024]{2,1,0:T(8,128)(2,1)} %bitcast.295), calls=%async_computation.1 | async-start | bytes 8388608 | tf_op jit(solution)/shard_map/all_to_all | solution.py:155
  192.0 233.7 %all-gather.12.cloned.1.call-start = ((), (), s32[]{:S(2)}) async-start(), calls=%async_computation.13 | async-start | bytes 5242880 | tf_op jit(solution)/shard_map/all_gather | solution.py:159
  241.1 53.7 %all-to-all-start.2 = ((bf16[32,64,1024]{2,1,0:T(8,128)(2,1)}), bf16[32,64,1024]{2,1,0:T(8,128)(2,1)}, u32[]{:S(2)}, u32[]{:S(2)}) async-start(bf16[32,64,1024]{2,1,0:T(8,128)(2,1)} %bitcast.310), calls=%async_computation.3 | async-start | bytes 8388608 | tf_op jit(solution)/shard_map/all_to_all | solution.py:191
  445.5 53.7 %all-to-all-start.1 = ((bf16[4,512,1024]{2,0,1:T(4,128)(2,1)}), bf16[4,512,1024]{2,0,1:T(4,128)(2,1)}, u32[]{:S(2)}, u32[]{:S(2)}) async-start(bf16[4,512,1024]{2,0,1:T(4,128)(2,1)} %copy.87), calls=%async_computation.2 | async-start | bytes 8388608 | tf_op jit(solution)/shard_map/all_to_all | solution.py:167
  499.2 53.7 %all-to-all-start.3 = ((bf16[4,512,1024]{2,0,1:T(4,128)(2,1)}), bf16[4,512,1024]{2,0,1:T(4,128)(2,1)}, u32[]{:S(2)}, u32[]{:S(2)}) async-start(bf16[4,512,1024]{2,0,1:T(4,128)(2,1)} %copy.93), calls=%async_computation.4 | async-start | bytes 8388608 | tf_op jit(solution)/shard_map/all_to_all | solution.py:223
  503.7 108.3 %all-gather.14.cloned.1.call-start = ((), (), s32[]{:S(2)}) async-start(), calls=%async_computation.14 | async-start | bytes 2621440 | tf_op jit(solution)/shard_map/all_gather | solution.py:238
  569.2 174.4 %all-reduce.11.cloned.1.call-start = ((), (), s32[]{:S(2)}) async-start(), calls=%async_computation.20 | async-start | bytes 3145728 | tf_op jit(solution)/shard_map/psum | solution.py:308
  618.3 58.9 %copy-start.19 = (f32[1024,64]{0,1:T(8,128)S(1)}, f32[1024,64]{0,1:T(8,128)}, u32[]{:S(2)}) copy-start(f32[1024,64]{0,1:T(8,128)} %get-tuple-element.330) | copy-start | bytes 786436
  685.3 136.7 %reduce-scatter.18.cloned.1.call-start = ((), (), s32[]{:S(2)}) async-start(), calls=%async_computation.19 | async-start | bytes 5242880
  706.7 195.0 %reduce-scatter.16.cloned.1.call-start = ((), (), s32[]{:S(2)}) async-start(), calls=%async_computation.18 | async-start | bytes 5242880
  729.6 251.6 %reduce-scatter.14.cloned.1.call-start = ((), (), s32[]{:S(2)}) async-start(), calls=%async_computation.17 | async-start | bytes 5242880 | tf_op jit(solution)/shard_map/reduce_scatter | solution.py:219
  737.9 290.0 %reduce-scatter.12.cloned.1.call-start = ((), (), s32[]{:S(2)}) async-start(), calls=%async_computation.15 | async-start | bytes 2621440 | tf_op jit(solution)/shard_map/reduce_scatter | solution.py:299
  742.6 413.2 %all-reduce.9.cloned.1.call-start = ((), (), s32[]{:S(2)}) async-start(), calls=%async_computation.16 | async-start | bytes 262144 | tf_op jit(solution)/shard_map/psum | solution.py:313
  904.6 123.4 %copy-start.7 = (bf16[256,1024]{1,0:T(8,128)(2,1)S(1)}, bf16[256,1024]{1,0:T(8,128)(2,1)}, u32[]{:S(2)}) copy-start(bf16[256,1024]{1,0:T(8,128)(2,1)} %param.19) | copy-start | bytes 1572868
  904.6 123.4 %copy-start.49 = (f32[1024]{0:T(1024)S(1)}, f32[1024]{0:T(1024)}, u32[]{:S(2)}) copy-start(f32[1024]{0:T(1024)} %param.23) | copy-start | bytes 12292
  904.6 123.4 %copy-start.57 = (f32[256]{0:T(256)S(1)}, f32[256]{0:T(256)}, u32[]{:S(2)}) copy-start(f32[256]{0:T(256)} %copy-done.56) | copy-start | bytes 3076
  906.0 123.4 %copy-start.59 = (f32[256]{0:T(256)S(1)}, f32[256]{0:T(256)}, u32[]{:S(2)}) copy-start(f32[256]{0:T(256)} %copy-done.58) | copy-start | bytes 3076
  906.0 123.4 %copy-start.5 = (f32[256,1024]{1,0:T(8,128)S(1)}, f32[256,1024]{1,0:T(8,128)}, u32[]{:S(2)}) copy-start(f32[256,1024]{1,0:T(8,128)} %copy-done.4) | copy-start | bytes 3145732
  906.0 123.4 %copy-start.11 = (f32[256,1024]{1,0:T(8,128)S(1)}, f32[256,1024]{1,0:T(8,128)}, u32[]{:S(2)}) copy-start(f32[256,1024]{1,0:T(8,128)} %copy-done.10) | copy-start | bytes 3145732
  906.0 123.5 %copy-start.48 = (f32[1024]{0:T(1024)S(1)}, f32[1024]{0:T(1024)}, u32[]{:S(2)}) copy-start(f32[1024]{0:T(1024)} %param.28) | copy-start | bytes 12292
  906.1 123.5 %copy-start.54 = (f32[256]{0:T(256)S(1)}, f32[256]{0:T(256)}, u32[]{:S(2)}) copy-start(f32[256]{0:T(256)} %copy-done.52) | copy-start | bytes 3076
  906.1 123.5 %copy-start.63 = (f32[256]{0:T(256)S(1)}, f32[256]{0:T(256)}, u32[]{:S(2)}) copy-start(f32[256]{0:T(256)} %copy-done.62) | copy-start | bytes 3076
  981.2 176.2 %copy-start.1 = (bf16[256,1024]{1,0:T(8,128)(2,1)S(1)}, bf16[256,1024]{1,0:T(8,128)(2,1)}, u32[]{:S(2)}) copy-start(bf16[256,1024]{1,0:T(8,128)(2,1)} %param.27) | copy-start | bytes 1572868
  (58 other events, 568.1 us)
Sparse Core Ops, SparseCore 0:
  10.8 48.6 all-gather.5
  106.7 75.4 reduce-scatter.9
  183.8 81.0 all-gather.9
  266.4 78.7 all-gather.7
  346.7 78.9 all-gather.11
  569.3 42.6 all-gather.13
  685.5 58.0 all-reduce.10
  745.8 76.1 reduce-scatter.17
  824.4 77.2 reduce-scatter.15
  903.8 77.2 reduce-scatter.13
  983.6 44.3 reduce-scatter.11
  1033.9 121.8 all-reduce.8
where the time goes:
time: 1180 us; the launch traced here: 1160 us
  waiting for transfers between devices  752 us (64%)
  matrix products  152 us (13%)
  local copies, waits for them, and re-layouts  113 us (10%)
  other arithmetic  63.7 us (5%)
  blocking collectives  39.6 us (3%)
  starting transfers between devices  19.4 us (2%)
  between operations  15.7 us (1%)
    unnamed x14, waiting for transfers between devices  148 us
    psum x1, waiting for transfers between devices, per_device(): lax.psum((grad_norm1, grad_norm2, grad_router), ('expert', 'tensor'))  83.3 us
    all_gather x1, waiting for transfers between devices, per_device(): lax.all_gather(w_down, 'tensor', axis=1, tiled=True)  72.7 us
    reduce_scatter x1, waiting for transfers between devices, per_device(): lax.psum_scatter(grad_down_w.astype(jnp.bfloat16), 'tensor', scatter_dime...  72.2 us
    reduce_scatter x1, waiting for transfers between devices, per_device(): lax.psum_scatter(jnp.dot(row_part, w_out, preferred_element_type=jnp.floa...  63.5 us
    unnamed x148, local copies, waits for them, and re-layouts  47.3 us
    all_gather x1, waiting for transfers between devices, per_device(): whole_rows = lax.all_gather(normed_one, 'tensor', axis=0, tiled=True)  44.2 us
    all_to_all x1, waiting for transfers between devices, per_device(): lax.all_to_all(grad_slots, 'expert', split_axis=0, concat_axis=1, tiled=T...  44 us
  transfers between devices with their start and end apart: 16, of which 14 were waited for; matrix products, arithmetic and copies ran while one was open for 15% of the time, Pallas kernels for 0%

commit v1 on v0

--- a/solution.py
+++ b/solution.py
@@ -1,6 +1,8 @@
 import jax
 import jax.numpy as jnp
 from jax import lax
+from jax.experimental import pallas as pl
+from jax.experimental.pallas import tpu as pltpu
 from jax.sharding import PartitionSpec as P
 
 HDIM = 64
@@ -43,7 +45,7 @@
     )
 
 
-def per_device(
+def per_device_slots(
     tokens,
     segment_ids,
     expert_ids,
@@ -329,9 +331,434 @@
     )
 
 
+ROW_BLOCK = 256
+VMEM_BYTES = 58 * 1024 * 1024
+GATHER_LIMIT = 32 * 1024 * 1024
+
+
+def dot_f32(left, right, left_dim, right_dim):
+    return lax.dot_general(
+        left,
+        right,
+        (((left_dim,), (right_dim,)), ((), ())),
+        preferred_element_type=jnp.float32,
+    )
+
+
+def half_swap(values):
+    width = values.shape[-1]
+    half = HDIM // 2
+    lane = lax.broadcasted_iota(jnp.int32, values.shape, 1)
+    ahead = pltpu.roll(values, width - half, 1)
+    behind = pltpu.roll(values, half, 1)
+    first = (lane % HDIM) < half
+    return jnp.where(first, ahead, behind), first
+
+
+def rope_rows(values, cos_table, sine_table):
+    swapped, first = half_swap(values)
+    return values * cos_table + jnp.where(first, -swapped, swapped) * sine_table
+
+
+def rope_rows_back(values, cos_table, sine_table):
+    swapped, first = half_swap(values * sine_table)
+    return values * cos_table + jnp.where(first, swapped, -swapped)
+
+
+def block_mask(seg_col, seg_row, start, rows, keys):
+    row_index = start + lax.broadcasted_iota(jnp.int32, (rows, keys), 0)
+    key_index = lax.broadcasted_iota(jnp.int32, (rows, keys), 1)
+    return (row_index >= key_index) & (seg_col[start : start + rows, :] == seg_row[:, :keys])
+
+
+def attention_forward(
+    q_raw, k_raw, values, cos_t, sin_t, seg_col, seg_row, heads_out, queries, keys_out
+):
+    length, q_width = q_raw.shape
+    k_width = k_raw.shape[1]
+    queries[...] = rope_rows(q_raw[...], cos_t[...], sin_t[...]).astype(jnp.bfloat16)
+    keys_out[...] = rope_rows(k_raw[...], cos_t[:, :k_width], sin_t[:, :k_width]).astype(
+        jnp.bfloat16
+    )
+    group = q_width // k_width
+    rows = min(length, ROW_BLOCK)
+    for start in range(0, length, rows):
+        count = start + rows
+        allowed = block_mask(seg_col, seg_row, start, rows, count)
+        for head in range(q_width // HDIM):
+            kv = head // group
+            q_blk = queries[start:count, head * HDIM : (head + 1) * HDIM]
+            k_blk = keys_out[:count, kv * HDIM : (kv + 1) * HDIM]
+            v_blk = values[:count, kv * HDIM : (kv + 1) * HDIM]
+            score = dot_f32(q_blk, k_blk, 1, 1) * ATTENTION_MULTIPLIER
+            score = jnp.where(allowed, score, MASKED)
+            weight = jnp.exp(score - jnp.max(score, axis=1, keepdims=True))
+            prob = weight * (1.0 / jnp.sum(weight, axis=1, keepdims=True))
+            out = dot_f32(prob.astype(jnp.bfloat16), v_blk, 1, 0)
+            heads_out[start:count, head * HDIM : (head + 1) * HDIM] = out.astype(jnp.bfloat16)
+
+
+def attention_backward(
+    queries, keys, values, grad_heads, cos_t, sin_t, seg_col, seg_row, dq_out, dk_out, dv_out, dq, dk, dv
+):
+    length, q_width = queries.shape
+    k_width = keys.shape[1]
+    group = q_width // k_width
+    rows = min(length, ROW_BLOCK)
+    dk[...] = jnp.zeros_like(dk)
+    dv[...] = jnp.zeros_like(dv)
+    for start in range(0, length, rows):
+        count = start + rows
+        allowed = block_mask(seg_col, seg_row, start, rows, count)
+        for head in range(q_width // HDIM):
+            kv = head // group
+            q_blk = queries[start:count, head * HDIM : (head + 1) * HDIM]
+            g_blk = grad_heads[start:count, head * HDIM : (head + 1) * HDIM]
+            k_blk = keys[:count, kv * HDIM : (kv + 1) * HDIM]
+            v_blk = values[:count, kv * HDIM : (kv + 1) * HDIM]
+            score = dot_f32(q_blk, k_blk, 1, 1) * ATTENTION_MULTIPLIER
+            score = jnp.where(allowed, score, MASKED)
+            weight = jnp.exp(score - jnp.max(score, axis=1, keepdims=True))
+            prob = weight * (1.0 / jnp.sum(weight, axis=1, keepdims=True))
+            grad_prob = dot_f32(g_blk, v_blk, 1, 1)
+            centre = jnp.sum(prob * grad_prob, axis=1, keepdims=True)
+            grad_score = (prob * (grad_prob - centre)).astype(jnp.bfloat16)
+            dq[start:count, head * HDIM : (head + 1) * HDIM] = (
+                dot_f32(grad_score, k_blk, 1, 0) * ATTENTION_MULTIPLIER
+            )
+            dk[:count, kv * HDIM : (kv + 1) * HDIM] += dot_f32(grad_score, q_blk, 0, 0)
+            dv[:count, kv * HDIM : (kv + 1) * HDIM] += dot_f32(
+                prob.astype(jnp.bfloat16), g_blk, 0, 0
+            )
+    dq_out[...] = rope_rows_back(dq[...], cos_t[...], sin_t[...]).astype(jnp.bfloat16)
+    dk_out[...] = rope_rows_back(
+        dk[...] * ATTENTION_MULTIPLIER, cos_t[:, :k_width], sin_t[:, :k_width]
+    ).astype(jnp.bfloat16)
+    dv_out[...] = dv[...].astype(jnp.bfloat16)
+
+
+def expert_kernel(
+    h2, dz, eid, loc, router, w_gu, w_dn, moe, dh2, grad_gu, grad_dn, grad_rt, xs, zs, ys, ds, hot, gate_s
+):
+    blocks, top, rows = eid.shape
+    experts = router.shape[0]
+    local_experts, _, double_hidden = w_gu.shape
+    hidden_width = double_hidden // 2
+    slots = hot.shape[1]
+    cap = slots // local_experts
+
+    @pl.when(pl.program_id(0) == 0)
+    def _():
+        grad_gu[...] = jnp.zeros_like(grad_gu)
+        grad_dn[...] = jnp.zeros_like(grad_dn)
+        grad_rt[...] = jnp.zeros_like(grad_rt)
+
+    slot_index = lax.broadcasted_iota(jnp.int32, (slots, rows), 0)
+    expert_index = lax.broadcasted_iota(jnp.int32, (experts, rows), 0)
+    gates = []
+    for b in range(blocks):
+        h_blk = h2[b * rows : (b + 1) * rows, :]
+        z_blk = dz[b * rows : (b + 1) * rows, :]
+        logits = dot_f32(router[...], h_blk, 1, 1)
+        chosen = [
+            jnp.sum(
+                jnp.where(expert_index == eid[b, k : k + 1, :], logits, 0.0), axis=0, keepdims=True
+            )
+            for k in range(top)
+        ]
+        peak = chosen[0]
+        for k in range(1, top):
+            peak = jnp.maximum(peak, chosen[k])
+        powers = [jnp.exp(c - peak) for c in chosen]
+        total = powers[0]
+        for k in range(1, top):
+            total = total + powers[k]
+        gate = [p / total for p in powers]
+        gates.append(gate)
+        weighted = jnp.zeros((slots, rows), jnp.float32)
+        chosen_hot = jnp.zeros((slots, rows), jnp.float32)
+        for k in range(top):
+            hit = slot_index == loc[b, k : k + 1, :]
+            weighted = jnp.where(hit, gate[k], weighted)
+            chosen_hot = jnp.where(hit, 1.0, chosen_hot)
+        hot_b = chosen_hot.astype(jnp.bfloat16)
+        hot[b] = hot_b
+        gate_s[b] = jnp.sum(weighted, axis=1, keepdims=True)
+        xs[b] = dot_f32(hot_b, h_blk, 1, 0).astype(jnp.bfloat16)
+        zs[b] = dot_f32(hot_b, z_blk, 1, 0).astype(jnp.bfloat16)
+    slot_grads = []
+    for e in range(local_experts):
+        span = slice(e * cap, (e + 1) * cap)
+        x_e = xs[:, span, :].reshape(blocks * cap, -1)
+        z_e = zs[:, span, :].reshape(blocks * cap, -1)
+        gate_e = gate_s[:, span, :].reshape(blocks * cap, 1)
+        both = dot_f32(x_e, w_gu[e], 1, 0)
+        g_act, u_act = both[:, :hidden_width], both[:, hidden_width:]
+        sig = 1.0 / (1.0 + jnp.exp(-g_act))
+        swish = g_act * sig
+        hid_f = swish * u_act
+        hid = hid_f.astype(jnp.bfloat16)
+        out = dot_f32(hid, w_dn[e], 1, 0)
+        ys[:, span, :] = (gate_e * out).astype(jnp.bfloat16).reshape(blocks, cap, -1)
+        grad_raw = dot_f32(z_e, w_dn[e], 1, 1) * RESIDUAL
+        slot_grads.append(
+            jnp.sum(hid.astype(jnp.float32) * grad_raw, axis=1, keepdims=True).reshape(
+                blocks, cap, 1
+            )
+        )
+        grad_hid = gate_e * grad_raw
+        dg = grad_hid * u_act * (sig * (1.0 + g_act * (1.0 - sig)))
+        du = grad_hid * swish
+        dgu = jnp.concatenate([dg, du], axis=1).astype(jnp.bfloat16)
+        scaled = (hid.astype(jnp.float32) * (gate_e * RESIDUAL)).astype(jnp.bfloat16)
+        grad_dn[e] += dot_f32(scaled, z_e, 0, 0)
+        grad_gu[e] += dot_f32(x_e, dgu, 0, 0)
+        ds[:, span, :] = dot_f32(dgu, w_gu[e], 1, 1).astype(jnp.bfloat16).reshape(blocks, cap, -1)
+    for b in range(blocks):
+        h_blk = h2[b * rows : (b + 1) * rows, :]
+        hot_b = hot[b]
+        moe[b * rows : (b + 1) * rows, :] = dot_f32(hot_b, ys[b], 0, 0).astype(jnp.bfloat16)
+        slot_grad = jnp.concatenate([part[b] for part in slot_grads], axis=0)
+        gate = gates[b]
+        grad_gate = [
+            jnp.sum(
+                jnp.where(slot_index == loc[b, k : k + 1, :], slot_grad, 0.0),
+                axis=0,
+                keepdims=True,
+            )
+            for k in range(top)
+        ]
+        centre = gate[0] * grad_gate[0]
+        for k in range(1, top):
+            centre = centre + gate[k] * grad_gate[k]
+        grad_logits = jnp.zeros((experts, rows), jnp.float32)
+        for k in range(top):
+            grad_logits = jnp.where(
+                expert_index == eid[b, k : k + 1, :],
+                gate[k] * (grad_gate[k] - centre),
+                grad_logits,
+            )
+        grad_logits = grad_logits.astype(jnp.bfloat16)
+        dh2[b * rows : (b + 1) * rows, :] = (
+            dot_f32(hot_b, ds[b], 0, 0) + dot_f32(grad_logits, router[...], 0, 0)
+        ).astype(jnp.bfloat16)
+        grad_rt[...] += dot_f32(grad_logits, h_blk, 1, 0)
+
+
+def whole_spec():
+    return pl.BlockSpec(memory_space=pltpu.VMEM)
+
+
+def per_device_tokens(
+    tokens,
+    segment_ids,
+    expert_ids,
+    slot_ids,
+    norm1_gain,
+    w_query,
+    w_key,
+    w_value,
+    w_out,
+    norm2_gain,
+    w_router,
+    w_gate,
+    w_up,
+    w_down,
+    cotangent,
+):
+    rows_dev, width = tokens.shape
+    top = expert_ids.shape[1]
+    experts = w_router.shape[1]
+    cap = rows_dev * top // experts
+    local_experts = w_gate.shape[0]
+    hidden_width = w_gate.shape[2]
+    length = segment_ids.shape[0]
+    per_seq = length // rows_dev
+    seqs = experts // local_experts
+    q_width, k_width = w_query.shape[1], w_key.shape[1]
+    bf16, f32 = jnp.bfloat16, jnp.float32
+    params = pltpu.CompilerParams(vmem_limit_bytes=VMEM_BYTES)
+
+    x_all_b = lax.all_gather(tokens, "tensor", axis=0, tiled=True)
+    w_out_in, x_all_b = lax.optimization_barrier((w_out, x_all_b))
+    w_out_all = lax.all_gather(w_out_in, "tensor", axis=0, tiled=True)
+    cot_in, w_out_all = lax.optimization_barrier((cotangent, w_out_all))
+    cot_seq = lax.all_gather(cot_in, "tensor", axis=0, tiled=True)
+    cot_all = lax.all_gather(cot_seq, "expert", axis=0, tiled=True)
+    code = (expert_ids * (cap + 1) + slot_ids + 1).T.reshape(1, top, rows_dev)
+    code = lax.all_gather(code, "tensor", axis=0, tiled=True)
+    code = lax.all_gather(code, "expert", axis=0, tiled=True)
+    eid = code // (cap + 1)
+    slot = code - eid * (cap + 1) - 1
+    first_slot = lax.axis_index("expert") * (local_experts * cap)
+    loc = jnp.where(slot >= 0, eid * cap + slot - first_slot, -1)
+    w_gu = jnp.concatenate([w_gate, w_up], axis=2)
+    router_t = w_router.T
+
+    x_all = x_all_b.astype(f32)
+    r1 = lax.rsqrt(jnp.mean(x_all * x_all, axis=-1, keepdims=True) + EPSILON)
+    h1 = (x_all * r1 * norm1_gain).astype(bf16)
+    cos_table, sine_table = rope_tables(jnp.arange(length).astype(f32), HDIM)
+    cos_t = jnp.tile(cos_table[:, 0, :], (1, q_width // HDIM))
+    sin_t = jnp.tile(sine_table[:, 0, :], (1, q_width // HDIM))
+    seg_col, seg_row = segment_ids[:, None], segment_ids[None, :]
+    q_raw = jnp.dot(h1, w_query, preferred_element_type=f32)
+    k_raw = jnp.dot(h1, w_key, preferred_element_type=f32)
+    values = jnp.dot(h1, w_value, preferred_element_type=f32).astype(bf16)
+    heads_out, queries, keys = pl.pallas_call(
+        attention_forward,
+        out_shape=(
+            jax.ShapeDtypeStruct((length, q_width), bf16),
+            jax.ShapeDtypeStruct((length, q_width), bf16),
+            jax.ShapeDtypeStruct((length, k_width), bf16),
+        ),
+        in_specs=[whole_spec()] * 7,
+        out_specs=(whole_spec(),) * 3,
+        compiler_params=params,
+        cost_estimate=pl.CostEstimate(
+            flops=6 * length * length * q_width, bytes_accessed=8 * length * q_width, transcendentals=length * length * 4
+        ),
+        name="attention_forward",
+    )(q_raw, k_raw, values, cos_t, sin_t, seg_col, seg_row)
+    heads_all = lax.all_gather(heads_out, "tensor", axis=1, tiled=True)
+    y_all = x_all + RESIDUAL * jnp.dot(heads_all, w_out_all, preferred_element_type=f32)
+    r2_all = lax.rsqrt(jnp.mean(y_all * y_all, axis=-1, keepdims=True) + EPSILON)
+    h2_seq = (y_all * r2_all * norm2_gain).astype(bf16)
+    h2_all = lax.all_gather(h2_seq, "expert", axis=0, tiled=True)
+
+    slots = local_experts * cap
+    total_rows = seqs * length
+    moe_part, dh2_part, grad_gu, grad_dn, grad_rt = pl.pallas_call(
+        expert_kernel,
+        grid=(seqs,),
+        out_shape=(
+            jax.ShapeDtypeStruct((total_rows, width), bf16),
+            jax.ShapeDtypeStruct((total_rows, width), bf16),
+            jax.ShapeDtypeStruct((local_experts, width, 2 * hidden_width), f32),
+            jax.ShapeDtypeStruct((local_experts, hidden_width, width), f32),
+            jax.ShapeDtypeStruct((experts, width), f32),
+        ),
+        in_specs=[
+            pl.BlockSpec((length, width), lambda i: (i, 0)),
+            pl.BlockSpec((length, width), lambda i: (i, 0)),
+            pl.BlockSpec((per_seq, top, rows_dev), lambda i: (i, 0, 0)),
+            pl.BlockSpec((per_seq, top, rows_dev), lambda i: (i, 0, 0)),
+            pl.BlockSpec((experts, width), lambda i: (0, 0)),
+            pl.BlockSpec((local_experts, width, 2 * hidden_width), lambda i: (0, 0, 0)),
+            pl.BlockSpec((local_experts, hidden_width, width), lambda i: (0, 0, 0)),
+        ],
+        out_specs=(
+            pl.BlockSpec((length, width), lambda i: (i, 0)),
+            pl.BlockSpec((length, width), lambda i: (i, 0)),
+            pl.BlockSpec((local_experts, width, 2 * hidden_width), lambda i: (0, 0, 0)),
+            pl.BlockSpec((local_experts, hidden_width, width), lambda i: (0, 0, 0)),
+            pl.BlockSpec((experts, width), lambda i: (0, 0)),
+        ),
+        scratch_shapes=[
+            pltpu.VMEM((per_seq, slots, width), bf16),
+            pltpu.VMEM((per_seq, slots, width), bf16),
+            pltpu.VMEM((per_seq, slots, width), bf16),
+            pltpu.VMEM((per_seq, slots, width), bf16),
+            pltpu.VMEM((per_seq, slots, rows_dev), bf16),
+            pltpu.VMEM((per_seq, slots, 1), f32),
+        ],
+        compiler_params=params,
+        cost_estimate=pl.CostEstimate(
+            flops=40 * 10**9, bytes_accessed=8 * total_rows * width, transcendentals=0
+        ),
+        name="experts",
+    )(h2_all, cot_all, eid, loc, router_t, w_gu, w_down)
+
+    dh2 = lax.psum_scatter(dh2_part, "expert", scatter_dimension=0, tiled=True)
+    moe_in, dh2 = lax.optimization_barrier((moe_part, dh2))
+    dh2 = lax.psum_scatter(dh2, "tensor", scatter_dimension=0, tiled=True).astype(f32)
+    moe = lax.psum_scatter(moe_in, "expert", scatter_dimension=0, tiled=True)
+
+    row_start = lax.axis_index("tensor") * rows_dev
+    y_own = lax.dynamic_slice_in_dim(y_all, row_start, rows_dev, 0)
+    r2 = lax.rsqrt(jnp.mean(y_own * y_own, axis=-1, keepdims=True) + EPSILON)
+    n2 = y_own * r2
+    upstream = cotangent.astype(f32)
+    grad_norm2 = jnp.sum(dh2 * n2, axis=0)
+    dn = dh2 * norm2_gain
+    dy = upstream + r2 * (dn - n2 * jnp.mean(dn * n2, axis=-1, keepdims=True))
+    grad_attn = lax.all_gather((RESIDUAL * dy).astype(bf16), "tensor", axis=0, tiled=True)
+    moe_late, grad_attn = lax.optimization_barrier((moe, grad_attn))
+    moe_own = lax.psum_scatter(moe_late, "tensor", scatter_dimension=0, tiled=True).astype(f32)
+    mixed = (y_own + RESIDUAL * moe_own).astype(bf16)
+    grad_rt = lax.psum(grad_rt, ("expert", "tensor"))
+
+    grad_heads = dot_f32(grad_attn, w_out, 1, 1).astype(bf16)
+    grad_out_w = contract_rows(heads_out, grad_attn).astype(bf16)
+    dq_raw, dk_raw, dv_raw = pl.pallas_call(
+        attention_backward,
+        out_shape=(
+            jax.ShapeDtypeStruct((length, q_width), bf16),
+            jax.ShapeDtypeStruct((length, k_width), bf16),
+            jax.ShapeDtypeStruct((length, k_width), bf16),
+        ),
+        in_specs=[whole_spec()] * 8,
+        out_specs=(whole_spec(),) * 3,
+        scratch_shapes=[
+            pltpu.VMEM((length, q_width), f32),
+            pltpu.VMEM((length, k_width), f32),
+            pltpu.VMEM((length, k_width), f32),
+        ],
+        compiler_params=params,
+        cost_estimate=pl.CostEstimate(
+            flops=12 * length * length * q_width, bytes_accessed=8 * length * q_width, transcendentals=length * length * 4
+        ),
+        name="attention_backward",
+    )(queries, keys, values, grad_heads, cos_t, sin_t, seg_col, seg_row)
+    summed = dot_f32(dq_raw, w_query, 1, 1) + dot_f32(dk_raw, w_key, 1, 1)
+    summed = summed + dot_f32(dv_raw, w_value, 1, 1)
+    dh1 = lax.psum_scatter(
+        summed.astype(bf16), "tensor", scatter_dimension=0, tiled=True
+    ).astype(f32)
+    grad_norm1 = jnp.sum(summed * (x_all * r1), axis=0)
+    grad_norm1, grad_norm2 = lax.psum((grad_norm1, grad_norm2), ("expert", "tensor"))
+    grad_q, grad_k, grad_v, grad_out_w = lax.psum(
+        (
+            contract_rows(h1, dq_raw).astype(bf16),
+            contract_rows(h1, dk_raw).astype(bf16),
+            contract_rows(h1, dv_raw).astype(bf16),
+            grad_out_w,
+        ),
+        "expert",
+    )
+    x_own = tokens.astype(f32)
+    r1_own = lax.rsqrt(jnp.mean(x_own * x_own, axis=-1, keepdims=True) + EPSILON)
+    n1 = x_own * r1_own
+    dn1 = dh1 * norm1_gain
+    grad_input = dy + r1_own * (dn1 - n1 * jnp.mean(dn1 * n1, axis=-1, keepdims=True))
+    return (
+        mixed,
+        grad_input,
+        grad_norm1,
+        grad_q.astype(f32),
+        grad_k.astype(f32),
+        grad_v.astype(f32),
+        grad_out_w.astype(f32),
+        grad_norm2,
+        grad_rt.T,
+        grad_gu[:, :, :hidden_width],
+        grad_gu[:, :, hidden_width:],
+        grad_dn,
+    )
+
+
+def choose_plan(mesh):
+    def per_device(tokens, *rest):
+        gathered = tokens.size * 2 * mesh.shape["expert"] * mesh.shape["tensor"]
+        plan = per_device_tokens if gathered <= GATHER_LIMIT else per_device_slots
+        return plan(tokens, *rest)
+
+    return per_device
+
+
 def solution(mesh):
     return jax.shard_map(
-        per_device,
+        choose_plan(mesh),
         mesh=mesh,
         in_specs=(
             P(("expert", "tensor"), None),

time: 1180 us -> 1120 us (0.949)
  Pallas kernels: 0 us -> 125 us
  matrix products: 152 us -> 29.5 us
  local copies, waits for them, and re-layouts: 113 us -> 16.3 us
  waiting for transfers between devices: 752 us -> 840 us
  other arithmetic: 63.7 us -> 24 us
  blocking collectives: 39.6 us -> 62.9 us
  starting transfers between devices: 19.4 us -> 0.96 us
    reduce_scatter x3 -> x5, waiting for transfers between devices: 180 us -> 363 us  [the longest x1 119 us: per_device_tokens(): moe = lax.psum_scatter(moe_in, 'expert', scatter_dimension=0, tiled=True)]
    unnamed x14, waiting for transfers between devices: 148 us -> 2.09 us
    all_gather x5 -> x7, waiting for transfers between devices: 197 us -> 343 us  [the longest x1 91.6 us: per_device_tokens(): cot_all = lax.all_gather(cot_seq, 'expert', axis=0, tiled=True)]
    all_to_all x4 -> x0, waiting for transfers between devices: 144 us -> none  [the longest x1 44 us: per_device(): lax.all_to_all(grad_slots, 'expert', split_axis=0, concat_axis=1, tiled=T...]
    pallas_call x0 -> x3, Pallas kernels: none -> 125 us  [the longest x1 83 us: per_device_tokens(): pl.pallas_call(expert_kernel, grid=(seqs,), out_shape=(jax.ShapeDtypeStru...]
    dot_general x35 -> x8, matrix products: 129 us -> 23.5 us  [the longest x4 13.5 us: dot_f32(): lax.dot_general(left, right, (((left_dim,), (right_dim,)), ((), ())), pre...]
    psum x2, waiting for transfers between devices: 83.4 us -> 132 us  [the longest x1 124 us: per_device_tokens(): grad_rt = lax.psum(grad_rt, ('expert', 'tensor'))]
    unnamed x148 -> x47, local copies, waits for them, and re-layouts: 47.3 us -> 5.63 us
  transfers between devices with their start and end apart: 16 -> 14, of which waited for: 14 -> 14; matrix products, arithmetic and copies ran while one was open for 15% -> 4% of each run, Pallas kernels for 0% -> 2%
where the time goes in v1:
time: 1120 us; the launch traced here: 1110 us
  waiting for transfers between devices  840 us (75%)
  Pallas kernels  125 us (11%)
  blocking collectives  62.9 us (6%)
  matrix products  29.5 us (3%)
  other arithmetic  24 us (2%)
  local copies, waits for them, and re-layouts  16.3 us (1%)
  between operations  14.3 us (1%)
    psum x1, waiting for transfers between devices, per_device_tokens(): grad_rt = lax.psum(grad_rt, ('expert', 'tensor'))  124 us
    reduce_scatter x1, waiting for transfers between devices, per_device_tokens(): moe = lax.psum_scatter(moe_in, 'expert', scatter_dimension=0, tiled=True)  119 us
    reduce_scatter x1, waiting for transfers between devices, per_device_tokens(): dh2 = lax.psum_scatter(dh2_part, 'expert', scatter_dimension=0, tiled=True)  116 us
    all_gather x1, waiting for transfers between devices, per_device_tokens(): cot_all = lax.all_gather(cot_seq, 'expert', axis=0, tiled=True)  91.6 us
    pallas_call x1, Pallas kernels, per_device_tokens(): pl.pallas_call(expert_kernel, grid=(seqs,), out_shape=(jax.ShapeDtypeStru...  83 us
    all_gather x1, waiting for transfers between devices, per_device_tokens(): h2_all = lax.all_gather(h2_seq, 'expert', axis=0, tiled=True)  64.3 us
    all_gather x1, waiting for transfers between devices, per_device_tokens(): x_all_b = lax.all_gather(tokens, 'tensor', axis=0, tiled=True)  50.3 us
    all_gather x1, waiting for transfers between devices, per_device_tokens(): heads_all = lax.all_gather(heads_out, 'tensor', axis=1, tiled=True)  47 us
  transfers between devices with their start and end apart: 14, of which 14 were waited for; matrix products, arithmetic and copies ran while one was open for 4% of the time, Pallas kernels for 2%

profile of v1, /device:TPU:0, one launch (start us, length us, event | category | flops | bytes accessed | tf_op | source)
XLA Modules:
  0.0 1113.5 jit_solution(16585007066477600163)
XLA Ops:
  8.0 50.3 %all-gather.9.cloned.1.call-done = bf16[1024,1024]{1,0:T(8,128)(2,1)} async-done(((bf16[256,1024]{1,0:T(8,128)(2,1)}), bf16[1024,1024]{1,0:T(8,128)(2,1)}) %all-gather.9.cloned.1.call-update) | async-done | bytes 2097168 | tf_op jit(solution)/shard_map/all_gather | solution.py:582
  61.5 2.5 copy.36.sin_t
  72.4 23.5 %attention_forward.1 = (bf16[1024,256]{1,0:T(8,128)(2,1)}, bf16[1024,256]{1,0:T(8,128)(2,1)}, bf16[1024,128]{1,0:T(8,128)(2,1)}) custom-call(f32[1024,256]{1,0:T(8,128)} %fusion.20.q_raw, f32[1024,128]{1,0:T(8,128)} %fusion.21.k_raw, bf16[1024,128]{1,0:T(8,128)(2,1)} %convolution_convert_fusion.5.values, f32[1024,256]{1,0:T(8,128)} %copy.35.cos_t, ...), custom_call_target="tpu_custom_call" | custom-call | flops 1610612736 | bytes 2097152 | tf_op jit(solution)/shard_map/attention_forward/pallas_call | solution.py:608
  96.0 8.5 all-gather.13.cloned.1.call-done
  104.6 47.0 %all-gather.11.cloned.1.call-done = bf16[1024,1024]{1,0:T(8,128)(2,1)} async-done(((bf16[1024,256]{1,0:T(8,128)(2,1)}), bf16[1024,1024]{1,0:T(8,128)(2,1)}) %all-gather.11.cloned.1.call-update) | async-done | bytes 2097168 | tf_op jit(solution)/shard_map/all_gather | solution.py:623
  151.6 5.4 multiply_reduce_fusion
  157.0 2.0 copy-done.4
  160.8 36.5 %all-gather.17.cloned.1.call-done = bf16[1024,1024]{1,0:T(8,128)(2,1)} async-done(((bf16[256,1024]{1,0:T(8,128)(2,1)}), bf16[1024,1024]{1,0:T(8,128)(2,1)}) %all-gather.17.cloned.1.call-update) | async-done | bytes 2097168 | tf_op jit(solution)/shard_map/all_gather | solution.py:586
  197.4 13.1 %all-gather = s32[32,256]{1,0:T(8,128)S(1)} all-gather(s32[8,256]{1,0:T(8,128)S(1)} %add_bitcast_fusion), channel_id=2, replica_groups=mesh['expert'=8,'tensor'=4] {'tensor'}, dimensions={0}, use_global_device_ids=true | all-gather | bytes 40960 | tf_op jit(solution)/shard_map/all_gather | solution.py:589
  210.5 10.3 all_gather.34
  220.8 3.1 pad_maximum_fusion.w_gu
  224.9 64.3 %all-gather.15.cloned.1.call-done.h2 = bf16[8192,1024]{1,0:T(8,128)(2,1)} async-done(((bf16[1024,1024]{1,0:T(8,128)(2,1)}), bf16[8192,1024]{1,0:T(8,128)(2,1)}) %all-gather.15.cloned.1.call-update) | async-done | bytes 16777232 | tf_op jit(solution)/shard_map/all_gather | solution.py:627
  289.2 91.6 %all-gather.19.cloned.1.call-done.dz = bf16[8192,1024]{1,0:T(8,128)(2,1)} async-done(((bf16[1024,1024]{1,0:T(8,128)(2,1)}), bf16[8192,1024]{1,0:T(8,128)(2,1)}) %all-gather.19.cloned.1.call-update) | async-done | bytes 16777232 | tf_op jit(solution)/shard_map/all_gather | solution.py:587
  380.9 83.0 %experts.1 = (bf16[8192,1024]{1,0:T(8,128)(2,1)}, bf16[8192,1024]{1,0:T(8,128)(2,1)}, f32[4,1024,256]{2,1,0:T(8,128)}, f32[4,128,1024]{2,1,0:T(8,128)}, f32[32,1024]{1,0:T(8,128)}) custom-call(bf16[8192,1024]{1,0:T(8,128)(2,1)} %all-gather.15.cloned.1.call-done.h2, bf16[8192,1024]{1,0:T(8,128)(2,1)} %all-gather.19.cloned.1.call-done.dz, ...), custom_call_target="tpu_custom_call" | custom-call | flops 40000000000 | bytes 67108864 | tf_op jit(solution)/shard_map/experts/pallas_call | solution.py:631
  463.9 116.1 %reduce-scatter.6.cloned.1.call-done = bf16[1024,1024]{1,0:T(8,128)(2,1)} async-done(((bf16[8192,1024]{1,0:T(8,128)(2,1)}), bf16[1024,1024]{1,0:T(8,128)(2,1)}) %reduce-scatter.6.cloned.1.call-update) | async-done | bytes 2097168 | tf_op jit(solution)/shard_map/reduce_scatter | solution.py:672
  581.5 44.7 %reduce-scatter.10.cloned.1.call-done = bf16[256,1024]{1,0:T(8,128)(2,1)} async-done(((bf16[1024,1024]{1,0:T(8,128)(2,1)}), bf16[256,1024]{1,0:T(8,128)(2,1)}) %reduce-scatter.10.cloned.1.call-update) | async-done | bytes 524304 | tf_op jit(solution)/shard_map/reduce_scatter | solution.py:674
  628.0 2.5 multiply_convert_fusion.1
  631.6 44.4 %all-gather.21.cloned.1.call-done = bf16[1024,1024]{1,0:T(8,128)(2,1)} async-done(((bf16[256,1024]{1,0:T(8,128)(2,1)}), bf16[1024,1024]{1,0:T(8,128)(2,1)}) %all-gather.21.cloned.1.call-update) | async-done | bytes 2097168 | tf_op jit(solution)/shard_map/all_gather | solution.py:685
  676.0 118.5 %reduce-scatter.8.cloned.1.call-done = bf16[1024,1024]{1,0:T(8,128)(2,1)} async-done(((bf16[8192,1024]{1,0:T(8,128)(2,1)}), bf16[1024,1024]{1,0:T(8,128)(2,1)}) %reduce-scatter.8.cloned.1.call-update) | async-done | bytes 2097168 | tf_op jit(solution)/shard_map/reduce_scatter | solution.py:675
  794.5 3.2 convolution_convert_fusion.2.grad_heads
  797.7 18.9 %attention_backward.1 = (bf16[1024,256]{1,0:T(8,128)(2,1)}, bf16[1024,128]{1,0:T(8,128)(2,1)}, bf16[1024,128]{1,0:T(8,128)(2,1)}) custom-call(bf16[1024,256]{1,0:T(8,128)(2,1)} %get-tuple-element.41.queries, bf16[1024,128]{1,0:T(8,128)(2,1)} %get-tuple-element.42.keys, bf16[1024,128]{1,0:T(8,128)(2,1)} %convolution_convert_fusion.5.values, ...), custom_call_target="tpu_custom_call" | custom-call | flops 3221225472 | bytes 2097152 | tf_op jit(solution)/shard_map/attention_backward/pallas_call | solution.py:693
  816.7 3.8 fusion.22
  826.8 1.9 fusion.23
  828.7 4.6 fusion.3
  834.5 4.6 fusion.19
  839.1 39.5 %all-reduce = (f32[1024]{0:T(1024)}, f32[1024]{0:T(1024)}) all-reduce(f32[1024]{0:T(1024)S(1)} %get-tuple-element.60, f32[1024]{0:T(1024)S(1)} %get-tuple-element.50), channel_id=1, replica_groups=mesh['expert'=8,'tensor'=4] {'expert','tensor'}, use_global_device_ids=true, to_apply=%region_12.13 | all-reduce | flops 2048 | bytes 16384 | tf_op jit(solution)/shard_map/psum | solution.py:719
  878.6 7.8 all-reduce.7.cloned.1.call-done
  886.4 2.2 convert_element_type.91
  892.4 39.5 %reduce-scatter.14.cloned.1.call-done = bf16[256,1024]{1,0:T(8,128)(2,1)} async-done(((bf16[1024,1024]{1,0:T(8,128)(2,1)}), bf16[256,1024]{1,0:T(8,128)(2,1)}) %reduce-scatter.14.cloned.1.call-update) | async-done | bytes 524304 | tf_op jit(solution)/shard_map/reduce_scatter | solution.py:715
  933.3 44.2 %reduce-scatter.12.cloned.1.call-done = bf16[256,1024]{1,0:T(8,128)(2,1)} async-done(((bf16[1024,1024]{1,0:T(8,128)(2,1)}), bf16[256,1024]{1,0:T(8,128)(2,1)}) %reduce-scatter.12.cloned.1.call-update) | async-done | bytes 524304 | tf_op jit(solution)/shard_map/reduce_scatter | solution.py:687
  977.5 3.3 fusion.12
  980.7 124.5 %all-reduce.5.cloned.1.call-done = f32[1024,32]{0,1:T(8,128)} async-done(((f32[1024,32]{0,1:T(8,128)}), f32[1024,32]{0,1:T(8,128)}) %all-reduce.5.cloned.1.call-update) | async-done | bytes 131088 | tf_op jit(solution)/shard_map/psum | solution.py:689
  (107 shorter events, 33.8 us)
Async XLA Ops:
  7.2 63.5 %copy-start = (bf16[1024,256]{1,0:T(8,128)(2,1)S(1)}, bf16[1024,256]{1,0:T(8,128)(2,1)}, u32[]{:S(2)}) copy-start(bf16[1024,256]{1,0:T(8,128)(2,1)} %param.20) | copy-start | bytes 1572868
  7.2 51.1 %all-gather.9.cloned.1.call-start = ((), (), s32[]{:S(2)}) async-start(), calls=%async_computation.5 | async-start | bytes 2621440 | tf_op jit(solution)/shard_map/all_gather | solution.py:582
  7.9 96.6 %all-gather.13.cloned.1.call-start = ((), (), s32[]{:S(2)}) async-start(), calls=%async_computation.7 | async-start | bytes 2621440 | tf_op jit(solution)/shard_map/all_gather | solution.py:584
  58.3 93.3 %all-gather.11.cloned.1.call-start = ((), (), s32[]{:S(2)}) async-start(), calls=%async_computation.6 | async-start | bytes 2621440 | tf_op jit(solution)/shard_map/all_gather | solution.py:623
  60.4 3.6 copy-start.22
  60.4 4.7 copy-start.1
  61.5 4.1 copy-start.19
  65.1 1.7 copy-start.2
  96.0 101.3 %all-gather.17.cloned.1.call-start = ((), (), s32[]{:S(2)}) async-start(), calls=%async_computation.9 | async-start | bytes 2621440 | tf_op jit(solution)/shard_map/all_gather | solution.py:586
  104.5 54.4 %copy-start.18 = (f32[1024]{0:T(1024)S(1)}, f32[1024]{0:T(1024)}, u32[]{:S(2)}) copy-start(f32[1024]{0:T(1024)} %param.24) | copy-start | bytes 12292
  104.6 184.7 %all-gather.15.cloned.1.call-start = ((), (), s32[]{:S(2)}) async-start(), calls=%async_computation.8 | async-start | bytes 18874368 | tf_op jit(solution)/shard_map/all_gather | solution.py:627
  157.0 2.0 copy-start.4
  160.7 36.6 %copy-start.20 = (s32[256,8]{0,1:T(8,128)S(1)}, s32[256,8]{0,1:T(8,128)}, u32[]{:S(2)}) copy-start(s32[256,8]{0,1:T(8,128)} %param.18) | copy-start | bytes 24580
  160.7 36.6 %copy-start.21 = (s32[256,8]{0,1:T(8,128)S(1)}, s32[256,8]{0,1:T(8,128)}, u32[]{:S(2)}) copy-start(s32[256,8]{0,1:T(8,128)} %param.17) | copy-start | bytes 24580
  160.7 220.1 %all-gather.19.cloned.1.call-start = ((), (), s32[]{:S(2)}) async-start(), calls=%async_computation.10 | async-start | bytes 18874368 | tf_op jit(solution)/shard_map/all_gather | solution.py:587
  197.3 382.7 %reduce-scatter.6.cloned.1.call-start = ((), (), s32[]{:S(2)}) async-start(), calls=%async_computation.11 | async-start | bytes 18874368 | tf_op jit(solution)/shard_map/reduce_scatter | solution.py:672
  463.9 162.3 %reduce-scatter.10.cloned.1.call-start = ((), (), s32[]{:S(2)}) async-start(), calls=%async_computation.13 | async-start | bytes 2621440 | tf_op jit(solution)/shard_map/reduce_scatter | solution.py:674
  580.0 48.0 %copy-start.7 = (bf16[256,1024]{1,0:T(8,128)(2,1)S(1)}, bf16[256,1024]{1,0:T(8,128)(2,1)}, u32[]{:S(2)}) copy-start(bf16[256,1024]{1,0:T(8,128)(2,1)} %param.29) | copy-start | bytes 1572868
  580.0 96.0 %all-gather.21.cloned.1.call-start = ((), (), s32[]{:S(2)}) async-start(), calls=%async_computation.14 | async-start | bytes 2621440 | tf_op jit(solution)/shard_map/all_gather | solution.py:685
  630.6 163.9 %reduce-scatter.8.cloned.1.call-start = ((), (), s32[]{:S(2)}) async-start(), calls=%async_computation.12 | async-start | bytes 18874368 | tf_op jit(solution)/shard_map/reduce_scatter | solution.py:675
  631.2 255.2 %all-reduce.7.cloned.1.call-start = ((), (), s32[]{:S(2)}) async-start(), calls=%async_computation.18 | async-start | bytes 3145728 | tf_op jit(solution)/shard_map/psum | solution.py:720
  816.7 3.8 copy-start.16
  820.5 1.6 copy-start.8
  820.5 1.7 copy-start.9
  826.7 2.0 copy-start.3
  826.7 105.2 %reduce-scatter.14.cloned.1.call-start = ((), (), s32[]{:S(2)}) async-start(), calls=%async_computation.16 | async-start | bytes 2621440 | tf_op jit(solution)/shard_map/reduce_scatter | solution.py:715
  826.7 1.9 copy-start.12
  833.3 144.2 %reduce-scatter.12.cloned.1.call-start = ((), (), s32[]{:S(2)}) async-start(), calls=%async_computation.15 | async-start | bytes 2621440 | tf_op jit(solution)/shard_map/reduce_scatter | solution.py:687
  834.0 271.2 %all-reduce.5.cloned.1.call-start = ((), (), s32[]{:S(2)}) async-start(), calls=%async_computation.17 | async-start | bytes 262144 | tf_op jit(solution)/shard_map/psum | solution.py:689
  886.4 4.0 copy-start.17
  886.4 4.8 copy-start.15
  888.6 88.9 %copy-start.6 = (bf16[256,1024]{1,0:T(8,128)(2,1)S(1)}, bf16[256,1024]{1,0:T(8,128)(2,1)}, u32[]{:S(2)}) copy-start(bf16[256,1024]{1,0:T(8,128)(2,1)} %reduce-scatter.10.cloned.1.call-done) | copy-start | bytes 1572868
  (5 other events, 6.4 us)
Sparse Core Ops, SparseCore 0:
  9.6 48.6 all-gather.8
  59.8 44.6 all-gather.12
  106.7 44.9 all-gather.10
  153.0 44.1 all-gather.16
  199.6 89.6 all-gather.14
  291.0 89.8 all-gather.18
  464.0 115.9 reduce-scatter.5
  582.3 43.8 reduce-scatter.9
  630.7 45.2 all-gather.20
  679.8 114.6 reduce-scatter.7
  826.8 59.5 all-reduce.6
  888.6 43.2 reduce-scatter.13
  934.3 43.1 reduce-scatter.11
  983.4 121.7 all-reduce.4

commit v2 on v1

--- a/solution.py
+++ b/solution.py
@@ -579,20 +579,44 @@
     bf16, f32 = jnp.bfloat16, jnp.float32
     params = pltpu.CompilerParams(vmem_limit_bytes=VMEM_BYTES)
 
+    tensors = per_seq
+    mine = lax.axis_index("tensor")
+    lane, place = mine % 2, mine // 2
+
+    def shifted(block, step):
+        return lax.ppermute(block, "tensor", [(i, (i + step) % tensors) for i in range(tensors)])
+
+    def weight_partner(block):
+        return lax.ppermute(block, "tensor", [(i, i ^ 1) for i in range(tensors)])
+
+    def token_partner(block):
+        return lax.ppermute(block, "tensor", [(i, i ^ 2) for i in range(tensors)])
+
+    def token_pair(block):
+        other = token_partner(block)
+        first = jnp.where(place == 0, block, other)
+        return jnp.concatenate([first, jnp.where(place == 0, other, block)], axis=0)
+
+    def gather_rows(block):
+        rows = block.shape[0]
+        parts = [shifted(block, step) for step in range(1, tensors)]
+        whole = jnp.zeros((tensors * rows, block.shape[1]), block.dtype)
+        for step, part in enumerate([block] + parts):
+            start = ((mine + tensors - step) % tensors) * rows
+            whole = lax.dynamic_update_slice_in_dim(whole, part, start, 0)
+        return whole
+
+    code = (expert_ids * (cap + 1) + slot_ids + 1).T.reshape(1, top, rows_dev)
+    code = lax.all_gather(token_pair(code), "expert", axis=0, tiled=True)
     x_all_b = lax.all_gather(tokens, "tensor", axis=0, tiled=True)
-    w_out_in, x_all_b = lax.optimization_barrier((w_out, x_all_b))
-    w_out_all = lax.all_gather(w_out_in, "tensor", axis=0, tiled=True)
-    cot_in, w_out_all = lax.optimization_barrier((cotangent, w_out_all))
-    cot_seq = lax.all_gather(cot_in, "tensor", axis=0, tiled=True)
-    cot_all = lax.all_gather(cot_seq, "expert", axis=0, tiled=True)
-    code = (expert_ids * (cap + 1) + slot_ids + 1).T.reshape(1, top, rows_dev)
-    code = lax.all_gather(code, "tensor", axis=0, tiled=True)
-    code = lax.all_gather(code, "expert", axis=0, tiled=True)
+    cot_pair = token_pair(cotangent)
+    w_out_in, cot_pair, code, x_all_b = lax.optimization_barrier((w_out, cot_pair, code, x_all_b))
+    w_out_all = gather_rows(w_out_in)
+    cot_all = lax.all_gather(cot_pair, "expert", axis=0, tiled=True)
     eid = code // (cap + 1)
     slot = code - eid * (cap + 1) - 1
     first_slot = lax.axis_index("expert") * (local_experts * cap)
     loc = jnp.where(slot >= 0, eid * cap + slot - first_slot, -1)
-    w_gu = jnp.concatenate([w_gate, w_up], axis=2)
     router_t = w_router.T
 
     x_all = x_all_b.astype(f32)
@@ -620,38 +644,53 @@
         ),
         name="attention_forward",
     )(q_raw, k_raw, values, cos_t, sin_t, seg_col, seg_row)
-    heads_all = lax.all_gather(heads_out, "tensor", axis=1, tiled=True)
+    heads_in, cot_all = lax.optimization_barrier((heads_out, cot_all))
+    heads_all = lax.all_gather(heads_in, "tensor", axis=1, tiled=True)
+    gate_in, up_in, down_in, heads_all, w_out_all = lax.optimization_barrier(
+        (w_gate, w_up, w_down, heads_all, w_out_all)
+    )
+    w_gu = jnp.concatenate(
+        [w_gate, weight_partner(gate_in), w_up, weight_partner(up_in)], axis=2
+    )
+    w_dn = jnp.concatenate([w_down, weight_partner(down_in)], axis=1)
     y_all = x_all + RESIDUAL * jnp.dot(heads_all, w_out_all, preferred_element_type=f32)
     r2_all = lax.rsqrt(jnp.mean(y_all * y_all, axis=-1, keepdims=True) + EPSILON)
     h2_seq = (y_all * r2_all * norm2_gain).astype(bf16)
-    h2_all = lax.all_gather(h2_seq, "expert", axis=0, tiled=True)
+    h2_pair = lax.dynamic_index_in_dim(
+        h2_seq.reshape(2, 2, rows_dev, width), lane, 1, keepdims=False
+    ).reshape(2 * rows_dev, width)
+    h2_all = lax.all_gather(h2_pair, "expert", axis=0, tiled=True)
 
     slots = local_experts * cap
-    total_rows = seqs * length
+    total_rows = seqs * 2 * rows_dev
+    per_step = per_seq
+    step_rows = per_step * rows_dev
+    wide = 2 * hidden_width
+    once = pl.Buffered(1)
     moe_part, dh2_part, grad_gu, grad_dn, grad_rt = pl.pallas_call(
         expert_kernel,
-        grid=(seqs,),
+        grid=(total_rows // step_rows,),
         out_shape=(
             jax.ShapeDtypeStruct((total_rows, width), bf16),
             jax.ShapeDtypeStruct((total_rows, width), bf16),
-            jax.ShapeDtypeStruct((local_experts, width, 2 * hidden_width), f32),
-            jax.ShapeDtypeStruct((local_experts, hidden_width, width), f32),
+            jax.ShapeDtypeStruct((local_experts, width, 2 * wide), f32),
+            jax.ShapeDtypeStruct((local_experts, wide, width), f32),
             jax.ShapeDtypeStruct((experts, width), f32),
         ),
         in_specs=[
-            pl.BlockSpec((length, width), lambda i: (i, 0)),
-            pl.BlockSpec((length, width), lambda i: (i, 0)),
-            pl.BlockSpec((per_seq, top, rows_dev), lambda i: (i, 0, 0)),
-            pl.BlockSpec((per_seq, top, rows_dev), lambda i: (i, 0, 0)),
+            pl.BlockSpec((step_rows, width), lambda i: (i, 0)),
+            pl.BlockSpec((step_rows, width), lambda i: (i, 0)),
+            pl.BlockSpec((per_step, top, rows_dev), lambda i: (i, 0, 0)),
+            pl.BlockSpec((per_step, top, rows_dev), lambda i: (i, 0, 0)),
             pl.BlockSpec((experts, width), lambda i: (0, 0)),
-            pl.BlockSpec((local_experts, width, 2 * hidden_width), lambda i: (0, 0, 0)),
-            pl.BlockSpec((local_experts, hidden_width, width), lambda i: (0, 0, 0)),
+            pl.BlockSpec((local_experts, width, 2 * wide), lambda i: (0, 0, 0), pipeline_mode=once),
+            pl.BlockSpec((local_experts, wide, width), lambda i: (0, 0, 0), pipeline_mode=once),
         ],
         out_specs=(
-            pl.BlockSpec((length, width), lambda i: (i, 0)),
-            pl.BlockSpec((length, width), lambda i: (i, 0)),
-            pl.BlockSpec((local_experts, width, 2 * hidden_width), lambda i: (0, 0, 0)),
-            pl.BlockSpec((local_experts, hidden_width, width), lambda i: (0, 0, 0)),
+            pl.BlockSpec((step_rows, width), lambda i: (i, 0)),
+            pl.BlockSpec((step_rows, width), lambda i: (i, 0)),
+            pl.BlockSpec((local_experts, width, 2 * wide), lambda i: (0, 0, 0), pipeline_mode=once),
+            pl.BlockSpec((local_experts, wide, width), lambda i: (0, 0, 0), pipeline_mode=once),
             pl.BlockSpec((experts, width), lambda i: (0, 0)),
         ),
         scratch_shapes=[
@@ -667,12 +706,19 @@
             flops=40 * 10**9, bytes_accessed=8 * total_rows * width, transcendentals=0
         ),
         name="experts",
-    )(h2_all, cot_all, eid, loc, router_t, w_gu, w_down)
-
-    dh2 = lax.psum_scatter(dh2_part, "expert", scatter_dimension=0, tiled=True)
-    moe_in, dh2 = lax.optimization_barrier((moe_part, dh2))
-    dh2 = lax.psum_scatter(dh2, "tensor", scatter_dimension=0, tiled=True).astype(f32)
-    moe = lax.psum_scatter(moe_in, "expert", scatter_dimension=0, tiled=True)
+    )(h2_all, cot_all, eid, loc, router_t, w_gu, w_dn)
+
+    def own_rows(pair):
+        kept = lax.dynamic_slice_in_dim(pair, place * rows_dev, rows_dev, 0)
+        sent = lax.dynamic_slice_in_dim(pair, (1 - place) * rows_dev, rows_dev, 0)
+        return kept.astype(f32) + token_partner(sent).astype(f32)
+
+    dh2_pair = lax.psum_scatter(dh2_part, "expert", scatter_dimension=0, tiled=True)
+    moe_in, grad_rt, grad_gu, grad_dn, dh2_pair = lax.optimization_barrier(
+        (moe_part, grad_rt, grad_gu, grad_dn, dh2_pair)
+    )
+    dh2 = own_rows(dh2_pair)
+    moe_pair = lax.psum_scatter(moe_in, "expert", scatter_dimension=0, tiled=True)
 
     row_start = lax.axis_index("tensor") * rows_dev
     y_own = lax.dynamic_slice_in_dim(y_all, row_start, rows_dev, 0)
@@ -682,11 +728,21 @@
     grad_norm2 = jnp.sum(dh2 * n2, axis=0)
     dn = dh2 * norm2_gain
     dy = upstream + r2 * (dn - n2 * jnp.mean(dn * n2, axis=-1, keepdims=True))
-    grad_attn = lax.all_gather((RESIDUAL * dy).astype(bf16), "tensor", axis=0, tiled=True)
-    moe_late, grad_attn = lax.optimization_barrier((moe, grad_attn))
-    moe_own = lax.psum_scatter(moe_late, "tensor", scatter_dimension=0, tiled=True).astype(f32)
-    mixed = (y_own + RESIDUAL * moe_own).astype(bf16)
-    grad_rt = lax.psum(grad_rt, ("expert", "tensor"))
+    grad_attn = gather_rows((RESIDUAL * dy).astype(bf16))
+    small = lax.psum(jnp.concatenate([grad_rt, grad_norm2[None, :]], axis=0), "expert")
+    small = lax.psum(small, "tensor")
+    grad_rt, grad_norm2 = small[:experts], small[experts]
+    gu_in, dn_in, grad_attn = lax.optimization_barrier((grad_gu, grad_dn, grad_attn))
+    grad_gate = gu_in[:, :, :hidden_width] + weight_partner(
+        gu_in[:, :, hidden_width:wide].astype(bf16)
+    ).astype(f32)
+    grad_up = gu_in[:, :, wide : wide + hidden_width] + weight_partner(
+        gu_in[:, :, wide + hidden_width :].astype(bf16)
+    ).astype(f32)
+    grad_down = dn_in[:, :hidden_width] + weight_partner(
+        dn_in[:, hidden_width:].astype(bf16)
+    ).astype(f32)
+    mixed = (y_own + RESIDUAL * own_rows(moe_pair)).astype(bf16)
 
     grad_heads = dot_f32(grad_attn, w_out, 1, 1).astype(bf16)
     grad_out_w = contract_rows(heads_out, grad_attn).astype(bf16)
@@ -712,11 +768,13 @@
     )(queries, keys, values, grad_heads, cos_t, sin_t, seg_col, seg_row)
     summed = dot_f32(dq_raw, w_query, 1, 1) + dot_f32(dk_raw, w_key, 1, 1)
     summed = summed + dot_f32(dv_raw, w_value, 1, 1)
-    dh1 = lax.psum_scatter(
-        summed.astype(bf16), "tensor", scatter_dimension=0, tiled=True
-    ).astype(f32)
-    grad_norm1 = jnp.sum(summed * (x_all * r1), axis=0)
-    grad_norm1, grad_norm2 = lax.psum((grad_norm1, grad_norm2), ("expert", "tensor"))
+    summed_b = summed.astype(bf16)
+    dh1 = lax.dynamic_slice_in_dim(summed, mine * rows_dev, rows_dev, 0)
+    for step in range(1, tensors):
+        start = ((mine + step) % tensors) * rows_dev
+        sent = lax.dynamic_slice_in_dim(summed_b, start, rows_dev, 0)
+        dh1 = dh1 + shifted(sent, step).astype(f32)
+    grad_norm1 = lax.psum(jnp.sum(summed * (x_all * r1), axis=0), ("expert", "tensor"))
     grad_q, grad_k, grad_v, grad_out_w = lax.psum(
         (
             contract_rows(h1, dq_raw).astype(bf16),
@@ -741,16 +799,17 @@
         grad_out_w.astype(f32),
         grad_norm2,
         grad_rt.T,
-        grad_gu[:, :, :hidden_width],
-        grad_gu[:, :, hidden_width:],
-        grad_dn,
+        grad_gate,
+        grad_up,
+        grad_down,
     )
 
 
 def choose_plan(mesh):
     def per_device(tokens, *rest):
         gathered = tokens.size * 2 * mesh.shape["expert"] * mesh.shape["tensor"]
-        plan = per_device_tokens if gathered <= GATHER_LIMIT else per_device_slots
+        fits = gathered <= GATHER_LIMIT and mesh.shape["tensor"] == 4
+        plan = per_device_tokens if fits else per_device_slots
         return plan(tokens, *rest)
 
     return per_device

time: 1120 us -> 823 us (0.73)
  waiting for transfers between devices: 840 us -> 468 us
  starting transfers between devices: 0.96 us -> 31.8 us
  Pallas kernels: 125 us -> 99.6 us
  blocking collectives: 62.9 us -> 87.4 us
  local copies, waits for them, and re-layouts: 16.3 us -> 39.7 us
  other arithmetic: 24 us -> 44.3 us
    all_gather x6 -> x3, waiting for transfers between devices: 292 us -> 49.4 us  [the longest x1 30.6 us: per_device_tokens(): cot_all = lax.all_gather(cot_pair, 'expert', axis=0, tiled=True)]
    reduce_scatter x5 -> x2, waiting for transfers between devices: 363 us -> 140 us  [the longest x1 70.6 us: per_device_tokens(): lax.psum_scatter(moe_in, 'expert', scatter_dimension=0, tiled=True)]
    ppermute x0 -> x19, waiting for transfers between devices: none -> 192 us  [the longest x4 70.8 us: token_partner(): return lax.ppermute(block, 'tensor', [(i, i ^ 2) for i in range(tensors)])]
    all_gather x1, waiting for transfers between devices: 50.3 us -> 0.01 us  [per_device_tokens(): x_all_b = lax.all_gather(tokens, 'tensor', axis=0, tiled=True)]
    psum x1 -> x2, waiting for transfers between devices: 124 us -> 86.1 us  [the longest x1 48.4 us: per_device_tokens(): lax.psum(jnp.concatenate([grad_rt, grad_norm2[None, :]], axis=0), 'expert')]
    psum x1, blocking collectives: 39.5 us -> 77.8 us  [per_device_tokens(): lax.psum(jnp.sum(summed * (x_all * r1), axis=0), ('expert', 'tensor'))]
    ppermute x0 -> x19, starting transfers between devices: none -> 31.5 us  [the longest x9 14.4 us: shifted(): lax.ppermute(block, 'tensor', [(i, (i + step) % tensors) for i in range(t...]
    pallas_call x1, Pallas kernels: 83 us -> 67.6 us  [per_device_tokens(): pl.pallas_call(expert_kernel, grid=(total_rows // step_rows,), out_shape=...]
  transfers between devices with their start and end apart: 14 -> 28, of which waited for: 14 -> 14; matrix products, arithmetic and copies ran while one was open for 4% -> 9% of each run, Pallas kernels for 2% -> 2%
where the time goes in v2:
time: 823 us; the launch traced here: 813 us
  waiting for transfers between devices  468 us (57%)
  Pallas kernels  99.6 us (12%)
  blocking collectives  87.4 us (11%)
  other arithmetic  44.3 us (5%)
  local copies, waits for them, and re-layouts  39.7 us (5%)
  starting transfers between devices  31.8 us (4%)
  matrix products  26.6 us (3%)
  between operations  14.6 us (2%)
    psum x1, blocking collectives, per_device_tokens(): lax.psum(jnp.sum(summed * (x_all * r1), axis=0), ('expert', 'tensor'))  77.8 us
    ppermute x4, waiting for transfers between devices, token_partner(): return lax.ppermute(block, 'tensor', [(i, i ^ 2) for i in range(tensors)])  70.8 us
    reduce_scatter x1, waiting for transfers between devices, per_device_tokens(): lax.psum_scatter(moe_in, 'expert', scatter_dimension=0, tiled=True)  70.6 us
    ppermute x6, waiting for transfers between devices, weight_partner(): return lax.ppermute(block, 'tensor', [(i, i ^ 1) for i in range(tensors)])  70.5 us
    reduce_scatter x1, waiting for transfers between devices, per_device_tokens(): lax.psum_scatter(dh2_part, 'expert', scatter_dimension=0, tiled=True)  69.6 us
    pallas_call x1, Pallas kernels, per_device_tokens(): pl.pallas_call(expert_kernel, grid=(total_rows // step_rows,), out_shape=...  67.6 us
    ppermute x9, waiting for transfers between devices, shifted(): lax.ppermute(block, 'tensor', [(i, (i + step) % tensors) for i in range(t...  50.6 us
    psum x1, waiting for transfers between devices, per_device_tokens(): lax.psum(jnp.concatenate([grad_rt, grad_norm2[None, :]], axis=0), 'expert')  48.4 us
  transfers between devices with their start and end apart: 28, of which 14 were waited for; matrix products, arithmetic and copies ran while one was open for 9% of the time, Pallas kernels for 2%

profile of v2, /device:TPU:0, one launch (start us, length us, event | category | flops | bytes accessed | tf_op | source)
XLA Modules:
  0.0 812.5 jit_solution(4002827934113498269)
XLA Ops:
  8.0 4.1 collective-permute-start
  12.8 48.5 %collective-permute-done.1 = s32[1,8,256]{2,1,0:T(8,128)S(1)} collective-permute-done((s32[1,8,256]{2,1,0:T(8,128)S(1)}, s32[1,8,256]{2,1,0:T(8,128)S(1)}, u32[]{:S(2)}, u32[]{:S(2)}) %collective-permute-start.1) | collective-permute-done | bytes 8224 | tf_op jit(solution)/shard_map/ppermute | solution.py:593
  61.3 9.6 %all_gather.15 = s32[16,8,256]{2,1,0:T(8,128)S(1)} all-gather(s32[2,8,256]{2,1,0:T(8,128)S(1)} %pad_add_fusion), channel_id=1, replica_groups=mesh['expert'=8,'tensor'=4] {'expert'}, dimensions={0}, use_global_device_ids=true | all-gather | bytes 147456 | tf_op jit(solution)/shard_map/all_gather | solution.py:610
  87.0 13.0 %attention_forward.1 = (bf16[1024,256]{1,0:T(8,128)(2,1)}, bf16[1024,256]{1,0:T(8,128)(2,1)}, bf16[1024,128]{1,0:T(8,128)(2,1)}) custom-call(f32[1024,256]{1,0:T(8,128)} %fusion.15.q_raw, f32[1024,128]{1,0:T(8,128)} %fusion.16.k_raw, bf16[1024,128]{1,0:T(8,128)(2,1)} %convolution_convert_fusion.5.values, f32[1024,256]{1,0:T(8,128)} %copy.35.cos_t, ...), custom_call_target="tpu_custom_call" | custom-call | flops 1610612736 | bytes 2097152 | tf_op jit(solution)/shard_map/attention_forward/pallas_call | solution.py:632
  100.0 30.6 %all-gather.7.cloned.1.call-done.dz = bf16[4096,1024]{1,0:T(8,128)(2,1)} async-done(((bf16[512,1024]{1,0:T(8,128)(2,1)}), bf16[4096,1024]{1,0:T(8,128)(2,1)}) %all-gather.7.cloned.1.call-update) | async-done | bytes 8388624 | tf_op jit(solution)/shard_map/all_gather | solution.py:615
  139.5 10.6 %collective-permute-done.2 = bf16[256,1024]{1,0:T(8,128)(2,1)} collective-permute-done((bf16[256,1024]{1,0:T(8,128)(2,1)}, bf16[256,1024]{1,0:T(8,128)(2,1)}, u32[]{:S(2)}, u32[]{:S(2)}) %collective-permute-start.2) | collective-permute-done | bytes 524320 | tf_op jit(solution)/shard_map/ppermute | solution.py:587
  152.0 40.0 %collective-permute-done.3 = bf16[256,1024]{1,0:T(8,128)(2,1)} collective-permute-done((bf16[256,1024]{1,0:T(8,128)(2,1)}, bf16[256,1024]{1,0:T(8,128)(2,1)}, u32[]{:S(2)}, u32[]{:S(2)}) %collective-permute-start.3) | collective-permute-done | bytes 524320 | tf_op jit(solution)/shard_map/ppermute | solution.py:587
  195.8 18.8 %all-gather.9.cloned.1.call-done = bf16[1024,1024]{1,0:T(8,128)(2,1)} async-done(((bf16[1024,256]{1,0:T(8,128)(2,1)}), bf16[1024,1024]{1,0:T(8,128)(2,1)}) %all-gather.9.cloned.1.call-update) | async-done | bytes 2097168 | tf_op jit(solution)/shard_map/all_gather | solution.py:648
  214.5 5.4 multiply_reduce_fusion
  227.8 21.6 %collective-permute-done.7 = bf16[4,128,1024]{2,1,0:T(8,128)(2,1)} collective-permute-done((bf16[4,128,1024]{2,1,0:T(8,128)(2,1)}, bf16[4,128,1024]{2,1,0:T(8,128)(2,1)}, u32[]{:S(2)}, u32[]{:S(2)}) %collective-permute-start.7) | collective-permute-done | bytes 1048608 | tf_op jit(solution)/shard_map/ppermute | solution.py:590
  249.4 3.7 pad_maximum_fusion.1.w_dn
  253.0 18.8 %collective-permute-done.5 = bf16[4,1024,128]{2,1,0:T(8,128)(2,1)} collective-permute-done((bf16[4,1024,128]{2,1,0:T(8,128)(2,1)}, bf16[4,1024,128]{2,1,0:T(8,128)(2,1)}, u32[]{:S(2)}, u32[]{:S(2)}) %collective-permute-start.5) | collective-permute-done | bytes 1048608 | tf_op jit(solution)/shard_map/ppermute | solution.py:590
  271.9 21.6 %collective-permute-done.6 = bf16[4,1024,128]{2,1,0:T(8,128)(2,1)} collective-permute-done((bf16[4,1024,128]{2,1,0:T(8,128)(2,1)}, bf16[4,1024,128]{2,1,0:T(8,128)(2,1)}, u32[]{:S(2)}, u32[]{:S(2)}) %collective-permute-start.6) | collective-permute-done | bytes 1048608 | tf_op jit(solution)/shard_map/ppermute | solution.py:590
  293.4 3.5 pad_maximum_fusion.w_gu
  296.9 67.6 %experts.1 = (bf16[4096,1024]{1,0:T(8,128)(2,1)}, bf16[4096,1024]{1,0:T(8,128)(2,1)}, f32[4,1024,512]{2,1,0:T(8,128)}, f32[4,256,1024]{2,1,0:T(8,128)}, f32[32,1024]{1,0:T(8,128)}) custom-call(bf16[4096,1024]{1,0:T(8,128)(2,1)} %all-gather.11.cloned.1.call-done.h2, bf16[4096,1024]{1,0:T(8,128)(2,1)} %all-gather.7.cloned.1.call-done.dz, ...), custom_call_target="tpu_custom_call" | custom-call | flops 40000000000 | bytes 33554432 | tf_op jit(solution)/shard_map/experts/pallas_call | solution.py:670
  364.6 69.6 %reduce-scatter.3.cloned.1.call-done = bf16[512,1024]{1,0:T(8,128)(2,1)} async-done(((bf16[4096,1024]{1,0:T(8,128)(2,1)}), bf16[512,1024]{1,0:T(8,128)(2,1)}) %reduce-scatter.3.cloned.1.call-update) | async-done | bytes 1048592 | tf_op jit(solution)/shard_map/reduce_scatter | solution.py:716
  438.6 70.6 %reduce-scatter.5.cloned.1.call-done = bf16[512,1024]{1,0:T(8,128)(2,1)} async-done(((bf16[4096,1024]{1,0:T(8,128)(2,1)}), bf16[512,1024]{1,0:T(8,128)(2,1)}) %reduce-scatter.5.cloned.1.call-update) | async-done | bytes 1048592 | tf_op jit(solution)/shard_map/reduce_scatter | solution.py:721
  514.9 22.3 %collective-permute-done.8 = bf16[256,1024]{1,0:T(8,128)(2,1)} collective-permute-done((bf16[256,1024]{1,0:T(8,128)(2,1)}, bf16[256,1024]{1,0:T(8,128)(2,1)}, u32[]{:S(2)}, u32[]{:S(2)}) %collective-permute-start.8) | collective-permute-done | bytes 524320 | tf_op jit(solution)/shard_map/ppermute | solution.py:593
  537.2 3.0 multiply_reduce_fusion.1
  541.8 3.2 constant_dynamic-update-slice_fusion.3
  546.4 3.4 collective-permute-start.11
  549.9 48.4 %all-reduce.5.cloned.1.call-done = f32[33,1024]{1,0:T(8,128)} async-done(((f32[33,1024]{1,0:T(8,128)}), f32[33,1024]{1,0:T(8,128)}) %all-reduce.5.cloned.1.call-update) | async-done | bytes 135184 | tf_op jit(solution)/shard_map/psum | solution.py:732
  598.4 37.7 %all-reduce.7.cloned.1.call-done = f32[33,1024]{1,0:T(8,128)} async-done(((f32[33,1024]{1,0:T(8,128)}), f32[33,1024]{1,0:T(8,128)}) %all-reduce.7.cloned.1.call-update) | async-done | bytes 135184 | tf_op jit(solution)/shard_map/psum | solution.py:733
  644.8 3.1 convolution_convert_fusion
  647.9 3.1 convolution_convert_fusion.2.grad_heads
  651.0 19.0 %attention_backward.1 = (bf16[1024,256]{1,0:T(8,128)(2,1)}, bf16[1024,128]{1,0:T(8,128)(2,1)}, bf16[1024,128]{1,0:T(8,128)(2,1)}) custom-call(bf16[1024,256]{1,0:T(8,128)(2,1)} %get-tuple-element.61.queries, bf16[1024,128]{1,0:T(8,128)(2,1)} %get-tuple-element.62.keys, bf16[1024,128]{1,0:T(8,128)(2,1)} %convolution_convert_fusion.5.values, ...), custom_call_target="tpu_custom_call" | custom-call | flops 3221225472 | bytes 2097152 | tf_op jit(solution)/shard_map/attention_backward/pallas_call | solution.py:749
  677.6 3.9 convert.7
  685.5 3.2 fusion.3
  697.9 77.8 %psum.49 = f32[1024]{0:T(1024)} all-reduce(f32[1024]{0:T(1024)S(1)} %get-tuple-element.85), channel_id=1, replica_groups=mesh['expert'=8,'tensor'=4] {'expert','tensor'}, use_global_device_ids=true, to_apply=%region_9.10 | all-reduce | flops 1024 | bytes 8192 | tf_op jit(solution)/shard_map/psum | solution.py:777
  780.0 3.1 fusion.10
  792.1 8.6 %collective-permute-done.17 = bf16[4,1024,128]{2,1,0:T(8,128)(2,1)S(1)} collective-permute-done((bf16[4,1024,128]{2,1,0:T(8,128)(2,1)}, bf16[4,1024,128]{2,1,0:T(8,128)(2,1)S(1)}, u32[]{:S(2)}, u32[]{:S(2)}) %collective-permute-start.17) | collective-permute-done | bytes 1048608 | tf_op jit(solution)/shard_map/ppermute | solution.py:590
  800.7 4.9 convert_add_fusion.2
  (161 shorter events, 95.7 us)
Async XLA Ops:
  7.2 78.1 %copy-start = (bf16[1024,256]{1,0:T(8,128)(2,1)S(1)}, bf16[1024,256]{1,0:T(8,128)(2,1)}, u32[]{:S(2)}) copy-start(bf16[1024,256]{1,0:T(8,128)(2,1)} %param.20) | copy-start | bytes 1572868
  7.2 65.8 %all-gather.5.cloned.1.call-start = ((), (), s32[]{:S(2)}) async-start(), calls=%async_computation.2 | async-start | bytes 2621440 | tf_op jit(solution)/shard_map/all_gather | solution.py:611
  7.9 122.7 %all-gather.7.cloned.1.call-start = ((), (), s32[]{:S(2)}) async-start(), calls=%async_computation.3 | async-start | bytes 9437184 | tf_op jit(solution)/shard_map/all_gather | solution.py:615
  8.0 62.9 %collective-permute-start = (bf16[256,1024]{1,0:T(8,128)(2,1)}, bf16[256,1024]{1,0:T(8,128)(2,1)S(1)}, u32[]{:S(2)}, u32[]{:S(2)}) collective-permute-start(bf16[256,1024]{1,0:T(8,128)(2,1)} %param.29), channel_id=1, source_target_pairs={{0,2},{1,3},{2,0},{3,1},{4,6},{5,7},{6,4},{7,5},{8,10},{9,11},{10,... | collective-permute-start | bytes 1572872 | tf_op jit(solution)/shard_map/ppermute | solution.py:593
  12.8 48.5 %collective-permute-start.1 = (s32[1,8,256]{2,1,0:T(8,128)S(1)}, s32[1,8,256]{2,1,0:T(8,128)S(1)}, u32[]{:S(2)}, u32[]{:S(2)}) collective-permute-start(s32[1,8,256]{2,1,0:T(8,128)S(1)} %add_bitcast_fusion), channel_id=1, source_target_pairs={{0,2},{1,3},{2,0},{3,1},{4,6},{5,7},{6,4},{7,5},{8,10},{9,11},{10,... | collective-permute-start | bytes 24584 | tf_op jit(solution)/shard_map/ppermute | solution.py:593
  73.1 141.5 %all-gather.9.cloned.1.call-start = ((), (), s32[]{:S(2)}) async-start(), calls=%async_computation.4 | async-start | bytes 2621440 | tf_op jit(solution)/shard_map/all_gather | solution.py:648
  130.6 166.3 %all-gather.11.cloned.1.call-start = ((), (), s32[]{:S(2)}) async-start(), calls=%async_computation.5 | async-start | bytes 9437184 | tf_op jit(solution)/shard_map/all_gather | solution.py:662
  130.7 19.5 %collective-permute-start.2 = (bf16[256,1024]{1,0:T(8,128)(2,1)}, bf16[256,1024]{1,0:T(8,128)(2,1)}, u32[]{:S(2)}, u32[]{:S(2)}) collective-permute-start(bf16[256,1024]{1,0:T(8,128)(2,1)} %param.23), channel_id=1, source_target_pairs={{0,1},{1,2},{2,3},{3,0},{4,5},{5,6},{6,7},{7,4},{8,9},{9,10},{10,1... | collective-permute-start | bytes 1572872 | tf_op jit(solution)/shard_map/ppermute | solution.py:587
  132.2 59.8 %collective-permute-start.3 = (bf16[256,1024]{1,0:T(8,128)(2,1)}, bf16[256,1024]{1,0:T(8,128)(2,1)}, u32[]{:S(2)}, u32[]{:S(2)}) collective-permute-start(bf16[256,1024]{1,0:T(8,128)(2,1)} %param.23), channel_id=1, source_target_pairs={{0,2},{1,3},{2,0},{3,1},{4,6},{5,7},{6,4},{7,5},{8,10},{9,11},{10,... | collective-permute-start | bytes 1572872 | tf_op jit(solution)/shard_map/ppermute | solution.py:587
  134.6 59.2 %collective-permute-start.4 = (bf16[256,1024]{1,0:T(8,128)(2,1)}, bf16[256,1024]{1,0:T(8,128)(2,1)}, u32[]{:S(2)}, u32[]{:S(2)}) collective-permute-start(bf16[256,1024]{1,0:T(8,128)(2,1)} %param.23), channel_id=1, source_target_pairs={{0,3},{1,0},{2,1},{3,2},{4,7},{5,4},{6,5},{7,6},{8,11},{9,8},{10,9... | collective-permute-start | bytes 1572872 | tf_op jit(solution)/shard_map/ppermute | solution.py:587
  222.9 211.3 %reduce-scatter.3.cloned.1.call-start = ((), (), s32[]{:S(2)}) async-start(), calls=%async_computation.6 | async-start | bytes 9437184 | tf_op jit(solution)/shard_map/reduce_scatter | solution.py:716
  223.0 26.4 %collective-permute-start.7 = (bf16[4,128,1024]{2,1,0:T(8,128)(2,1)}, bf16[4,128,1024]{2,1,0:T(8,128)(2,1)}, u32[]{:S(2)}, u32[]{:S(2)}) collective-permute-start(bf16[4,128,1024]{2,1,0:T(8,128)(2,1)} %param.28), channel_id=1, source_target_pairs={{0,1},{1,0},{2,3},{3,2},{4,5},{5,4},{6,7},{7,6},{8,9},{9,8},{10,11... | collective-permute-start | bytes 3145736 | tf_op jit(solution)/shard_map/ppermute | solution.py:590
  225.0 46.9 %collective-permute-start.5 = (bf16[4,1024,128]{2,1,0:T(8,128)(2,1)}, bf16[4,1024,128]{2,1,0:T(8,128)(2,1)}, u32[]{:S(2)}, u32[]{:S(2)}) collective-permute-start(bf16[4,1024,128]{2,1,0:T(8,128)(2,1)} %param.26), channel_id=1, source_target_pairs={{0,1},{1,0},{2,3},{3,2},{4,5},{5,4},{6,7},{7,6},{8,9},{9,8},{10,11... | collective-permute-start | bytes 3145736 | tf_op jit(solution)/shard_map/ppermute | solution.py:590
  225.1 68.4 %collective-permute-start.6 = (bf16[4,1024,128]{2,1,0:T(8,128)(2,1)}, bf16[4,1024,128]{2,1,0:T(8,128)(2,1)}, u32[]{:S(2)}, u32[]{:S(2)}) collective-permute-start(bf16[4,1024,128]{2,1,0:T(8,128)(2,1)} %param.27), channel_id=1, source_target_pairs={{0,1},{1,0},{2,3},{3,2},{4,5},{5,4},{6,7},{7,6},{8,9},{9,8},{10,11... | collective-permute-start | bytes 3145736 | tf_op jit(solution)/shard_map/ppermute | solution.py:590
  227.8 65.6 %copy-start.17 = (bf16[4,1024,128]{2,1,0:T(8,128)(2,1)S(1)}, bf16[4,1024,128]{2,1,0:T(8,128)(2,1)}, u32[]{:S(2)}) copy-start(bf16[4,1024,128]{2,1,0:T(8,128)(2,1)} %param.27) | copy-start | bytes 3145732
  227.8 65.6 %copy-start.18 = (bf16[4,1024,128]{2,1,0:T(8,128)(2,1)S(1)}, bf16[4,1024,128]{2,1,0:T(8,128)(2,1)}, u32[]{:S(2)}) copy-start(bf16[4,1024,128]{2,1,0:T(8,128)(2,1)} %param.26) | copy-start | bytes 3145732
  364.6 144.6 %reduce-scatter.5.cloned.1.call-start = ((), (), s32[]{:S(2)}) async-start(), calls=%async_computation.7 | async-start | bytes 9437184 | tf_op jit(solution)/shard_map/reduce_scatter | solution.py:721
  434.2 164.1 %all-reduce.5.cloned.1.call-start = ((), (), s32[]{:S(2)}) async-start(), calls=%async_computation.8 | async-start | bytes 327680 | tf_op jit(solution)/shard_map/psum | solution.py:732
  436.2 78.7 %collective-permute-start.9 = (bf16[256,1024]{1,0:T(8,128)(2,1)}, bf16[256,1024]{1,0:T(8,128)(2,1)S(1)}, u32[]{:S(2)}, u32[]{:S(2)}) collective-permute-start(bf16[256,1024]{1,0:T(8,128)(2,1)} %constant_dynamic-slice_fusion.3), channel_id=1, source_target_pairs={{0,2},{1,3},{2,0},{3,1},{4,6},{5,7},{6,4},{7,5},{8,10},{9,11},{10,... | collective-permute-start | bytes 1572872 | tf_op jit(solution)/shard_map/ppermute | solution.py:593
  511.1 26.1 %collective-permute-start.8 = (bf16[256,1024]{1,0:T(8,128)(2,1)}, bf16[256,1024]{1,0:T(8,128)(2,1)}, u32[]{:S(2)}, u32[]{:S(2)}) collective-permute-start(bf16[256,1024]{1,0:T(8,128)(2,1)} %constant_dynamic-slice_fusion.4), channel_id=1, source_target_pairs={{0,2},{1,3},{2,0},{3,1},{4,6},{5,7},{6,4},{7,5},{8,10},{9,11},{10,... | collective-permute-start | bytes 1572872 | tf_op jit(solution)/shard_map/ppermute | solution.py:593
  545.0 94.1 %collective-permute-start.10 = (bf16[256,1024]{1,0:T(8,128)(2,1)}, bf16[256,1024]{1,0:T(8,128)(2,1)}, u32[]{:S(2)}, u32[]{:S(2)}) collective-permute-start(bf16[256,1024]{1,0:T(8,128)(2,1)} %get-tuple-element.79), channel_id=1, source_target_pairs={{0,1},{1,2},{2,3},{3,0},{4,5},{5,6},{6,7},{7,4},{8,9},{9,10},{10,1... | collective-permute-start | bytes 1572872 | tf_op jit(solution)/shard_map/ppermute | solution.py:587
  546.2 89.9 %all-reduce.7.cloned.1.call-start = ((), (), s32[]{:S(2)}) async-start(), calls=%async_computation.9 | async-start | bytes 327680 | tf_op jit(solution)/shard_map/psum | solution.py:733
  546.4 94.5 %collective-permute-start.11 = (bf16[256,1024]{1,0:T(8,128)(2,1)}, bf16[256,1024]{1,0:T(8,128)(2,1)}, u32[]{:S(2)}, u32[]{:S(2)}) collective-permute-start(bf16[256,1024]{1,0:T(8,128)(2,1)} %get-tuple-element.79), channel_id=1, source_target_pairs={{0,2},{1,3},{2,0},{3,1},{4,6},{5,7},{6,4},{7,5},{8,10},{9,11},{10,... | collective-permute-start | bytes 1572872 | tf_op jit(solution)/shard_map/ppermute | solution.py:587
  549.8 93.0 %collective-permute-start.12 = (bf16[256,1024]{1,0:T(8,128)(2,1)}, bf16[256,1024]{1,0:T(8,128)(2,1)}, u32[]{:S(2)}, u32[]{:S(2)}) collective-permute-start(bf16[256,1024]{1,0:T(8,128)(2,1)} %get-tuple-element.79), channel_id=1, source_target_pairs={{0,3},{1,0},{2,1},{3,2},{4,7},{5,4},{6,5},{7,6},{8,11},{9,8},{10,9... | collective-permute-start | bytes 1572872 | tf_op jit(solution)/shard_map/ppermute | solution.py:587
  598.3 184.9 %all-reduce.9.cloned.1.call-start = ((), (), s32[]{:S(2)}) async-start(), calls=%async_computation.10 | async-start | bytes 3145728 | tf_op jit(solution)/shard_map/psum | solution.py:778
  676.2 113.0 %collective-permute-start.18 = (bf16[4,128,1024]{2,1,0:T(8,128)(2,1)}, bf16[4,128,1024]{2,1,0:T(8,128)(2,1)}, u32[]{:S(2)}, u32[]{:S(2)}) collective-permute-start(bf16[4,128,1024]{2,1,0:T(8,128)(2,1)} %slice.45), channel_id=1, source_target_pairs={{0,1},{1,0},{2,3},{3,2},{4,5},{5,4},{6,7},{7,6},{8,9},{9,8},{10,11... | collective-permute-start | bytes 3145736 | tf_op jit(solution)/shard_map/ppermute | solution.py:590
  683.2 108.9 %collective-permute-start.16 = (bf16[4,1024,128]{2,1,0:T(8,128)(2,1)}, bf16[4,1024,128]{2,1,0:T(8,128)(2,1)}, u32[]{:S(2)}, u32[]{:S(2)}) collective-permute-start(bf16[4,1024,128]{2,1,0:T(8,128)(2,1)} %get-tuple-element.84), channel_id=1, source_target_pairs={{0,1},{1,0},{2,3},{3,2},{4,5},{5,4},{6,7},{7,6},{8,9},{9,8},{10,11... | collective-permute-start | bytes 3145736 | tf_op jit(solution)/shard_map/ppermute | solution.py:590
  689.9 85.8 %collective-permute-start.13 = (bf16[256,1024]{1,0:T(8,128)(2,1)}, bf16[256,1024]{1,0:T(8,128)(2,1)}, u32[]{:S(2)}, u32[]{:S(2)}) collective-permute-start(bf16[256,1024]{1,0:T(8,128)(2,1)} %get-tuple-element.88), channel_id=1, source_target_pairs={{0,1},{1,2},{2,3},{3,0},{4,5},{5,6},{6,7},{7,4},{8,9},{9,10},{10,1... | collective-permute-start | bytes 1572872 | tf_op jit(solution)/shard_map/ppermute | solution.py:587
  691.3 86.6 %collective-permute-start.14 = (bf16[256,1024]{1,0:T(8,128)(2,1)}, bf16[256,1024]{1,0:T(8,128)(2,1)}, u32[]{:S(2)}, u32[]{:S(2)}) collective-permute-start(bf16[256,1024]{1,0:T(8,128)(2,1)} %get-tuple-element.90), channel_id=1, source_target_pairs={{0,2},{1,3},{2,0},{3,1},{4,6},{5,7},{6,4},{7,5},{8,10},{9,11},{10,... | collective-permute-start | bytes 1572872 | tf_op jit(solution)/shard_map/ppermute | solution.py:587
  692.6 85.3 %collective-permute-start.15 = (bf16[256,1024]{1,0:T(8,128)(2,1)}, bf16[256,1024]{1,0:T(8,128)(2,1)}, u32[]{:S(2)}, u32[]{:S(2)}) collective-permute-start(bf16[256,1024]{1,0:T(8,128)(2,1)} %get-tuple-element.89), channel_id=1, source_target_pairs={{0,3},{1,0},{2,1},{3,2},{4,7},{5,4},{6,5},{7,6},{8,11},{9,8},{10,9... | collective-permute-start | bytes 1572872 | tf_op jit(solution)/shard_map/ppermute | solution.py:587
  697.9 82.2 %copy-start.6 = (f32[256,1024]{1,0:T(8,128)S(1)}, f32[256,1024]{1,0:T(8,128)}, u32[]{:S(2)}) copy-start(f32[256,1024]{1,0:T(8,128)} %get-tuple-element.80) | copy-start | bytes 3145732
  775.7 25.0 %collective-permute-start.17 = (bf16[4,1024,128]{2,1,0:T(8,128)(2,1)}, bf16[4,1024,128]{2,1,0:T(8,128)(2,1)S(1)}, u32[]{:S(2)}, u32[]{:S(2)}) collective-permute-start(bf16[4,1024,128]{2,1,0:T(8,128)(2,1)} %get-tuple-element.83), channel_id=1, source_target_pairs={{0,1},{1,0},{2,3},{3,2},{4,5},{5,4},{6,7},{7,6},{8,9},{9,8},{10,11... | collective-permute-start | bytes 3145736 | tf_op jit(solution)/shard_map/ppermute | solution.py:590
  (23 other events, 169.7 us)
Sparse Core Ops, SparseCore 0:
  9.6 60.5 all-gather.4
  73.2 57.3 all-gather.6
  132.8 81.7 all-gather.8
  223.1 53.6 all-gather.10
  364.7 69.4 reduce-scatter.2
  437.9 71.2 reduce-scatter.4
  546.3 51.9 all-reduce.4
  600.6 35.4 all-reduce.6
  698.0 57.7 all-reduce.8
